TPU v7x, 32 devices: a whole 2x2x4 slice. The times are simulated.
32 devices in a mesh: seq: 8 (over z, y), ch: 4 (over x, core).
Axes of the slice: x: 2, y: 2, z: 4, core: 2. Of those that a mesh axis runs over, the one named last changes fastest.
Arguments:
- qkv: bfloat16 [3, 1024, 2048], P(None, 'seq', 'ch'), may hold values from -6 to 6
- filt: float32 [1024, 2048], P('seq', 'ch'), may hold values from -0.75 to 0.75
- skip_gain: float32 [2048], P('ch'), may hold values from -4 to 4
- short_weight: float32 [3, 3, 2048], P(None, None, 'ch'), may hold values from -3.5 to 3.5
- w_out: bfloat16 [2048, 2048], P(None, 'ch'), may hold values from -0.125 to 0.125
- g_out: bfloat16 [1024, 2048], P('seq', 'ch'), may hold values from -6 to 6
Outputs:
- output: bfloat16 [1024, 2048], P('seq', 'ch')
- grad_qkv: bfloat16 [3, 1024, 2048], P(None, 'seq', 'ch')
- grad_filter: float32 [1024, 2048], P('seq', 'ch')
All inputs are finite; a program needn't handle non-finite values.
Results may differ from a plain program's by a relative error of at most 0.0049.
Values may be sent and summed in bfloat16 or wider, within the bound.
No kernel may reach another device: no remote copies, remote signals or barrier semaphores. Data moves between devices by JAX's collectives and lax.ppermute only.
A program may use at most 64 MiB of HBM per device.

v0:
```python
import functools
import math

import jax
import jax.numpy as jnp
import numpy as np
from jax import lax
from jax.experimental import pallas as pl
from jax.experimental.pallas import tpu as pltpu
from jax.sharding import PartitionSpec as P

HIGHEST = lax.Precision.HIGHEST
TWO_PI = 2.0 * math.pi
LANES = 128
HALF = 64
PHASES = 4
STRIP = 16
BF16 = jnp.bfloat16
F32 = jnp.float32
VMEM_LIMIT = 24 * 1024 * 1024


def passed_along(block, axis, distance):
    devices = range(lax.axis_size(axis))
    route = [(i - distance, i) for i in devices if i - distance in devices]
    return lax.ppermute(block, axis, route)


def phase_pair(left_count, right_count, period, left_start, right_start):
    left_idx = lax.broadcasted_iota(jnp.int32, (left_count, right_count), 0) + left_start
    right_idx = lax.broadcasted_iota(jnp.int32, (left_count, right_count), 1) + right_start
    angle_all = (left_idx * right_idx % period).astype(jnp.float32) * (TWO_PI / period)
    return (jnp.cos(angle_all), jnp.sin(angle_all))


def contract(pattern, matrix, values):
    return jnp.einsum(
        pattern, matrix, values, precision=HIGHEST, preferred_element_type=jnp.float32
    )


def forward_spectrum(signal):
    seq_parts = lax.axis_size("seq")
    row_count = signal.shape[0]
    row_share = row_count // seq_parts
    period = 2 * seq_parts * row_count
    spread_in = lax.all_to_all(signal[None], "seq", split_axis=1, concat_axis=0, tiled=True)
    outer_cos, outer_sin = phase_pair(2 * seq_parts, seq_parts, 2 * seq_parts, 0, 0)
    section_re = contract("cp,prw->crw", outer_cos, spread_in)
    section_im = -contract("cp,prw->crw", outer_sin, spread_in)
    twist_cos, twist_sin = phase_pair(
        2 * seq_parts, row_share, period, 0, lax.axis_index("seq") * row_share
    )
    twist_cos = twist_cos[:, :, None]
    twist_sin = twist_sin[:, :, None]
    turned_re = section_re * twist_cos + section_im * twist_sin
    turned_im = section_im * twist_cos - section_re * twist_sin
    inner_cos, inner_sin = phase_pair(row_count, row_count, row_count, 0, 0)
    piece_re = lax.all_to_all(turned_re, "seq", split_axis=0, concat_axis=1, tiled=True)
    piece_im = lax.all_to_all(turned_im, "seq", split_axis=0, concat_axis=1, tiled=True)
    spec_re = contract("dm,cmk->cdk", inner_cos, piece_re) + contract(
        "dm,cmk->cdk", inner_sin, piece_im
    )
    spec_im = contract("dm,cmk->cdk", inner_cos, piece_im) - contract(
        "dm,cmk->cdk", inner_sin, piece_re
    )
    return (spec_re, spec_im)


def time_signal(spec_re, spec_im):
    seq_parts = lax.axis_size("seq")
    row_count = spec_re.shape[1]
    period = 2 * seq_parts * row_count
    inner_cos, inner_sin = phase_pair(row_count, row_count, row_count, 0, 0)
    back_re = contract("md,cdk->cmk", inner_cos, spec_re) - contract(
        "md,cdk->cmk", inner_sin, spec_im
    )
    back_im = contract("md,cdk->cmk", inner_cos, spec_im) + contract(
        "md,cdk->cmk", inner_sin, spec_re
    )
    twist_cos, twist_sin = phase_pair(2, row_count, period, 2 * lax.axis_index("seq"), 0)
    twist_cos = twist_cos[:, :, None]
    twist_sin = twist_sin[:, :, None]
    turned_re = back_re * twist_cos - back_im * twist_sin
    turned_im = back_im * twist_cos + back_re * twist_sin
    outer_cos, outer_sin = phase_pair(seq_parts, 2 * seq_parts, 2 * seq_parts, 0, 0)
    piece_re = lax.all_to_all(turned_re, "seq", split_axis=1, concat_axis=0, tiled=True)
    piece_im = lax.all_to_all(turned_im, "seq", split_axis=1, concat_axis=0, tiled=True)
    summed = contract("pc,crk->prk", outer_cos, piece_re) - contract(
        "pc,crk->prk", outer_sin, piece_im
    )
    returned = summed * (1.0 / period)
    return lax.all_to_all(returned, "seq", split_axis=0, concat_axis=1, tiled=True)[0]


def spread_layer(qkv, filt, skip_gain, short_weight, w_out, g_out):
    row_count = qkv.shape[1]
    slab_width = qkv.shape[2]
    tail_rows = passed_along(qkv[:, row_count - 2 :, :], "seq", 1)
    extended = jnp.concatenate([tail_rows, qkv], axis=1)
    short = (
        short_weight[:, 0, None, :] * extended[:, 2:, :]
        + short_weight[:, 1, None, :] * extended[:, 1:-1, :]
        + short_weight[:, 2, None, :] * extended[:, :-2, :]
    )
    query_gate = short[0]
    key_short = short[1]
    value_short = short[2]
    mixed = key_short * value_short
    both_re, both_im = forward_spectrum(jnp.concatenate([mixed, filt], axis=1))
    signal_re = both_re[:, :, :slab_width]
    signal_im = both_im[:, :, :slab_width]
    kernel_re = both_re[:, :, slab_width:]
    kernel_im = both_im[:, :, slab_width:]
    conv_out = time_signal(
        signal_re * kernel_re - signal_im * kernel_im, signal_re * kernel_im + signal_im * kernel_re
    )
    long_out = conv_out + skip_gain * mixed
    gated_out = (query_gate * long_out).astype(jnp.bfloat16)
    projected = jnp.dot(
        lax.all_gather(gated_out, "ch", axis=1, tiled=True),
        w_out,
        preferred_element_type=jnp.float32,
    )
    output = projected.astype(jnp.bfloat16)
    grad_all = lax.all_gather(g_out, "ch", axis=1, tiled=True)
    rows_all = lax.all_to_all(w_out, "ch", split_axis=0, concat_axis=1, tiled=True)
    grad_gated = lax.dot_general(
        grad_all, rows_all, (((1,), (1,)), ((), ())), preferred_element_type=jnp.float32
    )
    grad_long = grad_gated * query_gate
    grad_query = grad_gated * long_out
    grad_re, grad_im = forward_spectrum(grad_long)
    pair_re = jnp.concatenate(
        [kernel_re * grad_re + kernel_im * grad_im, signal_re * grad_re + signal_im * grad_im],
        axis=2,
    )
    pair_im = jnp.concatenate(
        [kernel_re * grad_im - kernel_im * grad_re, signal_re * grad_im - signal_im * grad_re],
        axis=2,
    )
    pair_time = time_signal(pair_re, pair_im)
    grad_mixed = pair_time[:, :slab_width] + skip_gain * grad_long
    token_total = lax.axis_size("seq") * row_count
    grad_filter = pair_time[:, slab_width:] * (1.0 / math.sqrt(token_total))
    grad_short = jnp.stack([grad_query, grad_mixed * value_short, grad_mixed * key_short])
    head_rows = passed_along(grad_short[:, :2, :], "seq", -1)
    extended_grad = jnp.concatenate([grad_short, head_rows], axis=1)
    grad_qkv = (
        short_weight[:, 0, None, :] * extended_grad[:, :-2, :]
        + short_weight[:, 1, None, :] * extended_grad[:, 1:-1, :]
        + short_weight[:, 2, None, :] * extended_grad[:, 2:, :]
    ).astype(jnp.bfloat16)
    return (output, grad_qkv, grad_filter)


def split_bf16(values):
    high = values.astype(np.float32).astype(jnp.bfloat16)
    low = (values - high.astype(np.float64)).astype(np.float32).astype(jnp.bfloat16)
    return high, low


def phase_tables(tokens):
    quarter = tokens // PHASES
    freq = 2 * np.arange(quarter)[:, None] + 1
    turn = math.pi / (2 * tokens)
    angle = (freq * PHASES * np.arange(quarter)[None, :] % (4 * tokens)) * turn
    forward = np.concatenate([np.cos(angle), -np.sin(angle)], axis=1)
    backward = np.concatenate([np.cos(angle).T, -np.sin(angle).T], axis=1) / tokens
    angle = freq * np.arange(PHASES)[None, :] * turn
    twist = np.concatenate([np.cos(angle), np.sin(angle)], axis=1)
    twist = np.pad(twist, ((0, 0), (0, LANES - 2 * PHASES)))
    high, rest = split_bf16(twist)
    last = split_bf16(twist - high.astype(np.float64) - rest.astype(np.float64))[0]
    tables = np.zeros((8, quarter, 2 * quarter), jnp.bfloat16)
    tables[0], tables[1] = split_bf16(forward)
    tables[2], tables[3] = split_bf16(backward)
    for i, term in enumerate((high, rest, last)):
        tables[4, :, i * LANES : (i + 1) * LANES] = term
    return tables


def row_order(rows, back=False):
    to, at = [lax.broadcasted_iota(jnp.int32, (rows, rows), int(i != back)) for i in range(2)]
    share = rows // PHASES
    wanted = (to & (share - 1)) * PHASES + lax.shift_right_logical(to, share.bit_length() - 1)
    return jnp.where(wanted == at, 1.0, 0.0).astype(BF16)


def mm(a, b):
    return lax.dot_general(a, b, (((1,), (0,)), ((), ())), preferred_element_type=F32)


def low_lanes(shape):
    return lax.broadcasted_iota(jnp.int32, shape, 1) < HALF


def swap(x):
    return pltpu.roll(x, HALF, 1)


class Near:
    def __init__(self, array, kept=False):
        self.array = array
        self.kept = kept


class Far:
    def __init__(self, array, cuts=None, turned=(), into=None, axis=0):
        self.array = array
        self.turned = turned
        self.into = into
        self.axis = axis
        if turned:
            step = array.shape[0] // len(turned)
            cuts = [(mask * step, step) for mask in turned]
        self.cuts = cuts or [(0, array.shape[axis])]
        self.shape = list(array.shape)
        self.shape[axis] = sum(count for _, count in self.cuts)


class Stage:
    def __init__(self, items, count_in, refs):
        arrays, scratch = list(refs[: len(items)]), list(refs[len(items) :])
        sems = scratch.pop()
        self.count_in = count_in
        self.held, self.copies, self.waiting = [], [], []
        used = 0
        for i, (item, array) in enumerate(zip(items, arrays)):
            group = []
            if isinstance(item, Near):
                self.held.append(array)
            else:
                held = scratch.pop(0) if item.into is None else arrays[count_in + item.into]
                self.held.append(held)
                at = 0
                for cut, (start, count) in enumerate(item.cuts):
                    lead = (slice(None),) * item.axis
                    there = held.at[(*lead, pl.ds(start if item.turned else at, count))]
                    at += count
                    if item.turned:
                        mask = item.turned[cut]
                        start = pl.multiple_of((lax.axis_index("ch") ^ mask) * count, count)
                    here = array.at[(*lead, pl.ds(start, count))]
                    if i >= count_in:
                        here, there = there, here
                    group.append(pltpu.make_async_copy(here, there, sems.at[used]))
                    used += 1
            self.copies.append(group)
            self.waiting.append(set(range(len(group))))
        self.given = set()

    def bring(self, index):
        for copy in self.copies[index]:
            copy.start()

    def take(self, index, cut=None):
        for i in sorted(self.waiting[index]):
            if cut is None or cut == i:
                self.copies[index][i].wait()
                self.waiting[index].discard(i)
        return self.held[index]

    def out(self, index):
        return self.held[self.count_in + index]

    def give(self, index, cut=None):
        for i, copy in enumerate(self.copies[self.count_in + index]):
            if (index, i) not in self.given and cut in (None, i):
                copy.start()
                self.given.add((index, i))


def staged(kernel, items, count_in, *refs):
    stage = Stage(items, count_in, refs)
    for i in range(count_in):
        stage.bring(i)
    kernel(stage)
    for i in range(count_in):
        stage.take(i)
    for i in range(len(items) - count_in):
        stage.give(i)
    for i in range(len(items) - count_in):
        stage.take(count_in + i)


def operand_of(x):
    if isinstance(x, Near) and not x.kept:
        return x.array
    space = pltpu.VMEM if isinstance(x, Near) else pltpu.HBM
    return pltpu.with_memory_space_constraint(x.array, space)


def result_of(x):
    make = pltpu.HBM if isinstance(x, Far) else pltpu.VMEM if x.kept else jax.ShapeDtypeStruct
    return make(x.array.shape, x.array.dtype)


def call(kernel, results, *args, flops=0):
    items = list(args) + list(results)
    specs, scratch, used = [], [], 0
    for item in items:
        near = isinstance(item, Near)
        specs.append(pl.BlockSpec(memory_space=pltpu.VMEM if near else pltpu.HBM))
        if not near:
            used += len(item.cuts)
            if item.into is None:
                scratch.append(pltpu.VMEM(tuple(item.shape), item.array.dtype))
    moved = sum(math.prod(x.array.shape) * x.array.dtype.itemsize for x in items)
    return pl.pallas_call(
        functools.partial(staged, kernel, items, len(args)),
        out_shape=[result_of(x) for x in results],
        in_specs=specs[: len(args)],
        out_specs=specs[len(args) :],
        scratch_shapes=scratch + [pltpu.SemaphoreType.DMA((max(used, 1),))],
        compiler_params=pltpu.CompilerParams(vmem_limit_bytes=VMEM_LIMIT),
        cost_estimate=pl.CostEstimate(flops=flops, bytes_accessed=moved, transcendentals=0),
    )(*[operand_of(x) for x in args])


def lane_tile(x, index):
    return x[:, index * LANES : (index + 1) * LANES]


def pair(first, second):
    low = low_lanes(first.shape)
    return jnp.where(low, first, swap(second)), jnp.where(low, swap(first), second)


def both(x):
    turned, low = swap(x), low_lanes(x.shape)
    return jnp.where(low, x, turned), jnp.where(low, turned, x)


def shifted(x, before):
    rows = lax.broadcasted_iota(jnp.int32, x.shape, 0)
    last, first = before[1:2, :], before[0:1, :]
    one = jnp.where(rows == 0, last, pltpu.roll(x, 1, 0))
    two = jnp.where(rows == 0, first, jnp.where(rows == 1, last, pltpu.roll(x, 2, 0)))
    return one, two


def advanced(x, after):
    count = x.shape[0]
    rows = lax.broadcasted_iota(jnp.int32, x.shape, 0)
    first, last = after[0:1, :], after[1:2, :]
    one = jnp.where(rows == count - 1, first, pltpu.roll(x, count - 1, 0))
    two = jnp.where(
        rows == count - 1, last, jnp.where(rows == count - 2, first, pltpu.roll(x, count - 2, 0))
    )
    return one, two


def put_rows(x, send_ref, at):
    half = x.shape[0] // 2
    for tile in range(x.shape[1] // LANES):
        t = lane_tile(x, tile)
        first, second = pair(t[:half], t[half:])
        send_ref[2 * tile, at : at + half] = first.astype(BF16)
        send_ref[2 * tile + 1, at : at + half] = second.astype(BF16)


def put_strip(x, send_ref, at):
    x = jnp.concatenate([x, jnp.zeros((STRIP - x.shape[0], x.shape[1]), F32)], axis=0)
    for tile in range(x.shape[1] // LANES):
        t = lane_tile(x, tile)
        send_ref[2 * tile, at : at + STRIP] = t.astype(BF16)
        send_ref[2 * tile + 1, at : at + STRIP] = swap(t).astype(BF16)


def strip_of(ref, at):
    tiles = []
    for tile in range(ref.shape[0] // 2):
        x, y = [ref[2 * tile + i, at : at + STRIP].astype(F32) for i in range(2)]
        tiles.append(jnp.where(low_lanes(x.shape), x, swap(y)))
    return jnp.concatenate(tiles, axis=1)


def exact_rows(x):
    high = x.astype(BF16).astype(F32)
    return jnp.concatenate([high, x - high], axis=0)


def group_rows(x):
    return lax.broadcasted_iota(jnp.int32, x.shape, 0) & 7


def earlier(x, count):
    return pltpu.roll(x, x.shape[0] - count, 0)


def strip_groups(ref, at, half):
    x = ref[:, at : at + STRIP, :].astype(F32)[:, 8 * half : 8 * half + 8, :]
    return x.reshape(8 * ref.shape[0], LANES)


def exact_groups(*halves):
    strips = []
    for x in halves:
        x = jnp.where(group_rows(x) < 2, x, 0.0)
        high = x.astype(BF16).astype(F32)
        strips.append((high + pltpu.roll(x - high, 2, 0)).reshape(x.shape[0] // 8, 8, LANES))
    return jnp.concatenate(strips, axis=1).astype(BF16)


def own_rows(x):
    none, last = jnp.zeros_like(x[:1]), x[x.shape[0] - 1 :]
    return jnp.concatenate([x[:2], none, x[:1], last, none, x[x.shape[0] - 2 :]], axis=0)


def first_rows(groups, weight):
    last = jnp.concatenate([jnp.zeros((8, LANES), F32), groups[: groups.shape[0] - 8]], axis=0)
    return (
        weight[0:1] * groups
        + weight[1:2] * (earlier(groups, 2) + earlier(last, 4))
        + weight[2:3] * earlier(last, 6)
    )


def short_of(x, weight):
    one, two = shifted(x, jnp.zeros((2, x.shape[1]), F32))
    return weight[0:1, :] * x + weight[1:2, :] * one + weight[2:3, :] * two


def adjoint_of(x, after, weight):
    one, two = advanced(x, after)
    return weight[0:1, :] * x + weight[1:2, :] * one + weight[2:3, :] * two


def start_kernel(stage):
    send_ref, weight_ref = stage.out(0), stage.take(0)
    qkv_ref = stage.take(1)
    rows = qkv_ref.shape[1]
    order = row_order(rows)
    query, key, value = [qkv_ref[i].astype(F32) for i in range(3)]
    put_strip(own_rows(query), send_ref, rows)
    key_rows, value_rows = own_rows(key), own_rows(value)
    mixed = short_of(key, weight_ref[1]) * short_of(value, weight_ref[2])
    mixed, taps = mm(order, mixed.astype(BF16)), mm(order, stage.take(2)[...].astype(BF16))
    for tile in range(mixed.shape[1] // LANES):
        strips = pair(lane_tile(key_rows, tile), lane_tile(value_rows, tile))
        parts = pair(lane_tile(mixed, tile), lane_tile(taps, tile))
        for i in range(2):
            send_ref[2 * tile + i, :rows] = parts[i].astype(BF16)
            raw = send_ref[2 * tile + i, rows:].astype(F32)
            raw = jnp.concatenate([raw[:8], strips[i]], axis=0)
            send_ref[2 * tile + i, rows:] = raw.astype(BF16)


def partial_product(g, w_ref, mask):
    width = g.shape[1]
    w = w_ref[mask * width : (mask + 1) * width, :]
    return lax.dot_general(g, w, (((1,), (1,)), ((), ())), preferred_element_type=F32)


def first_product_kernel(stage):
    g, out_ref = stage.take(0)[...], stage.out(0)
    for i, mask in enumerate((1, 3)):
        out_ref[i] = partial_product(g, stage.take(1, i), mask).astype(BF16)


def second_product_kernel(stage):
    w_ref, g, near_ref = stage.take(1), stage.take(0)[...], stage.take(2)
    across_ref, own_ref = stage.out(0), stage.out(1)
    across = partial_product(g, w_ref, 2) + near_ref[1].astype(F32)
    across_ref[...] = across.astype(BF16)
    stage.give(0)
    own_ref[...] = partial_product(g, w_ref, 0) + near_ref[0].astype(F32)


def query_kernel(stage):
    weight_ref, qkv_ref, short_ref = stage.take(1), stage.take(0), stage.out(4)
    for i in range(3):
        short_ref[i] = short_of(qkv_ref[i].astype(F32), weight_ref[i])
    stage.give(4)
    stage.out(3)[...] = short_ref[0]


def sum_kernel(stage):
    send_ref, kept_ref = stage.out(0), stage.out(1)
    grad_gated = stage.take(0)[...] + stage.take(1)[...].astype(F32)
    kept_ref[...] = grad_gated
    stage.give(1)
    rows = grad_gated.shape[0]
    first = exact_rows(grad_gated[:2])
    put_strip(jnp.concatenate([jnp.zeros_like(first), first], axis=0), send_ref, rows // 2)
    put_rows(mm(row_order(rows), (grad_gated * stage.take(2)[...]).astype(BF16)), send_ref, 0)


def spread_phases(parts):
    (a_re, a_im), (b_re, b_im), (c_re, c_im), (d_re, d_im) = parts
    s_re, s_im, t_re, t_im = a_re + c_re, a_im + c_im, a_re - c_re, a_im - c_im
    u_re, u_im, v_re, v_im = b_re + d_re, b_im + d_im, b_re - d_re, b_im - d_im
    return [
        (s_re + u_re, s_im + u_im),
        (t_re + v_im, t_im - v_re),
        (s_re - u_re, s_im - u_im),
        (t_re - v_im, t_im + v_re),
    ]


def gather_phases(parts):
    (a_re, a_im), (b_re, b_im), (c_re, c_im), (d_re, d_im) = parts
    s_re, s_im, t_re, t_im = a_re + c_re, a_im + c_im, a_re - c_re, a_im - c_im
    u_re, u_im, v_re, v_im = b_re + d_re, b_im + d_im, b_re - d_re, b_im - d_im
    return [
        (s_re + u_re, s_im + u_im),
        (t_re - v_im, t_im + v_re),
        (s_re - u_re, s_im - u_im),
        (t_re + v_im, t_im - v_re),
    ]


def rows_of(ref, start, count):
    block = ref[:, start : start + count, :]
    return block.reshape(ref.shape[0] * count, ref.shape[2])


def turned_back(re, im, twist, phase):
    if phase == 0:
        return re, im
    c, s = twist[:, phase : phase + 1], twist[:, PHASES + phase : PHASES + phase + 1]
    return re * c + im * s, im * c - re * s


def turned_on(re, im, twist, phase):
    if phase == 0:
        return re, im
    c, s = twist[:, phase : phase + 1], twist[:, PHASES + phase : PHASES + phase + 1]
    return re * c - im * s, re * s + im * c


def lane_tile(x, index):
    return x[:, index * LANES : (index + 1) * LANES]


def causal(parts, weight):
    rows = lax.broadcasted_iota(jnp.int32, parts[0].shape, 0)
    two, three = [jnp.where(rows == 0, 0.0, pltpu.roll(parts[p], 1, 0)) for p in (2, 3)]
    once, twice = [three, *parts[:3]], [two, three, *parts[:2]]
    return [
        weight[0:1] * x + weight[1:2] * y + weight[2:3] * z for x, y, z in zip(parts, once, twice)
    ]


def anticausal(parts, weight):
    count = parts[0].shape[0]
    rows = lax.broadcasted_iota(jnp.int32, parts[0].shape, 0)
    zero, one = [
        jnp.where(rows == count - 1, 0.0, pltpu.roll(parts[p], count - 1, 0)) for p in (0, 1)
    ]
    once, twice = [*parts[1:], zero], [*parts[2:], zero, one]
    return [
        weight[0:1] * x + weight[1:2] * y + weight[2:3] * z for x, y, z in zip(parts, once, twice)
    ]


def halves(x):
    high = x.astype(BF16)
    return high, (x - high.astype(F32)).astype(BF16)


def twiddles(table_ref):
    terms = [table_ref[2, :, i * LANES : (i + 1) * LANES].astype(F32) for i in range(3)]
    return terms[0] + (terms[1] + terms[2])


def columns(parts):
    return jnp.concatenate(parts, axis=1)


def two_sides(table, x):
    quarter = table.shape[0]
    return [mm(table[:, :quarter], x), mm(table[:, quarter:], x)]


def spectrum_of(sides, twist):
    turned = []
    for phase, (re, im) in enumerate(sides):
        turned.append(turned_back(re, im, twist, phase))
    return spread_phases(turned)


def back_values(spectrum, twist):
    return [
        jnp.concatenate(turned_on(re, im, twist, phase), axis=0)
        for phase, (re, im) in enumerate(gather_phases(spectrum))
    ]


def own_weights(weight_ref, gain_ref):
    place = lax.axis_index("seq")
    lanes = pl.ds(pl.multiple_of(place // 2 * LANES, LANES), LANES)
    odd = place % 2 == 1

    def mine(x):
        return jnp.where(odd, swap(x), x)

    query, key, value = [mine(weight_ref[i, :, lanes]) for i in range(3)]
    gain = both(mine(gain_ref[:, lanes]))[0]
    return jnp.where(low_lanes(key.shape), key, swap(value)), query, gain


def first_mask(quarter, share):
    rows = lax.broadcasted_iota(jnp.int32, (quarter, LANES), 0) & (share - 1)
    return (rows == 0) & low_lanes((quarter, LANES))


def spread_first(groups, index, share):
    x = groups.reshape(groups.shape[0] // 8, 8, LANES)[:, index : index + 1, :]
    return jnp.broadcast_to(x, (x.shape[0], share, LANES)).reshape(x.shape[0] * share, LANES)


def gather_first(parts, share):
    tops = []
    for x in parts:
        tops.append(
            jnp.concatenate([x[at : at + 8] for at in range(0, x.shape[0], share)], axis=0)
        )
    return jnp.where(group_rows(tops[0]) == 0, tops[0], pltpu.roll(tops[1], 1, 0))


def forward_kernel(stage):
    recv_ref, weight_ref, gain_ref = [stage.take(i) for i in range(3)]
    send_ref, saved_ref = stage.out(0), stage.out(1)
    blocks = recv_ref.shape[0]
    rows = recv_ref.shape[1] - STRIP
    share = rows // PHASES
    quarter = blocks * share
    low, starting = low_lanes((quarter, LANES)), first_mask(quarter, share)
    pair_weight, query_weight, gain = own_weights(weight_ref, gain_ref)
    query = first_rows(strip_groups(recv_ref, rows, 0), query_weight)
    pairs = first_rows(strip_groups(recv_ref, rows, 1), pair_weight)
    saved_ref[10, 8:9, :] = gain
    saved_ref[10, 64 : 64 + 8 * blocks, :] = query
    saved_ref[10, 128 : 128 + 8 * blocks, :] = pairs
    strip = exact_groups(query, pairs)
    fixed = pairs * swap(pairs)

    starts = [phase * share for phase in range(PHASES)]
    x = [rows_of(recv_ref, at, share).astype(F32) for at in starts]
    for i in range(2):
        x[i] = jnp.where(starting, spread_first(fixed, i, share), x[i])
    high = columns([y.astype(BF16) for y in x])
    fh, fl = stage.take(3)[0], stage.take(3)[1]
    twist = twiddles(stage.take(3))
    main = [y + z for y, z in zip(two_sides(fh, high), two_sides(fl, high))]
    sides = [[lane_tile(y, phase) for y in main] for phase in range(PHASES)]
    product = []
    for r, (re, im) in enumerate(spectrum_of(sides, twist)):
        saved_ref[2 * r] = re
        saved_ref[2 * r + 1] = im
        other_re, other_im = swap(re), swap(im)
        product.append((re * other_re - im * other_im, re * other_im + im * other_re))

    values = back_values(product, twist)
    bh, bl = stage.take(4)[0], stage.take(4)[1]
    wide = low_lanes((2 * quarter, LANES))
    high = [y.astype(BF16) for y in values]
    wider = [y.astype(F32) for y in high]
    both_parts = [jnp.where(wide, z, y - z).astype(BF16) for y, z in zip(values, wider)]
    high = [jnp.where(wide, wider[i], wider[i + 2]).astype(BF16) for i in range(2)]
    main, more = mm(bh, columns(both_parts)), mm(bl, columns(high))
    grad_ref = stage.take(5)
    send_ref[:, rows // 2 : rows, :] = grad_ref[:, : rows // 2, :]
    send_ref[:, rows:, :] = strip + grad_ref[:, rows // 2 :, :]
    stage.give(0, 1)
    summed = [y + swap(y) for y in (lane_tile(main, phase) for phase in range(PHASES))]
    for i in range(2):
        conv = jnp.where(low, summed[i], summed[i + 2]) + lane_tile(more, i)
        long_out = conv + gain * jnp.where(low, x[i], swap(x[i + 2]))
        saved_ref[8 + i] = long_out
        long_out = long_out.astype(BF16).reshape(blocks, share, LANES)
        send_ref[:, starts[i] : starts[i] + share, :] = long_out


def backward_kernel(stage):
    grad_ref, saved_ref, send_ref = stage.take(0), stage.take(1), stage.out(0)
    blocks = grad_ref.shape[0]
    rows = grad_ref.shape[1] - STRIP
    share = rows // PHASES
    quarter = blocks * share
    low, starting = low_lanes((quarter, LANES)), first_mask(quarter, share)
    gain, groups = saved_ref[10, 8:9, :], 8 * blocks
    query, pairs = [saved_ref[10, at : at + groups, :] for at in (64, 128)]
    strip = strip_groups(grad_ref, rows, 0)
    first = earlier(strip, 4) + earlier(strip, 6)
    fixed = first * query
    starts = [phase * share for phase in range(PHASES)]
    grad_long = []
    for i, at in enumerate(starts[2:]):
        packed = rows_of(grad_ref, at, share).astype(F32)
        grad_long.append(jnp.where(starting, spread_first(fixed, i, share), packed))

    fh, fl = stage.take(2)[0], stage.take(2)[1]
    twist = twiddles(stage.take(2))
    high, rest = halves(columns(grad_long))
    three = zip(two_sides(fh, high), two_sides(fl, high), two_sides(fh, rest))
    main = [x + y + z for x, y, z in three]
    sides = []
    for phase in range(PHASES):
        sides.append([both(lane_tile(x, phase % 2))[phase // 2] for x in main])
    product = []
    for r, (re, im) in enumerate(spectrum_of(sides, twist)):
        k_re, k_im = saved_ref[2 * r], saved_ref[2 * r + 1]
        product.append((k_re * re + k_im * im, k_re * im - k_im * re))
    high, rest = halves(columns(back_values(product, twist)))
    bh, bl = stage.take(3)[0], stage.take(3)[1]
    times = mm(bh, high) + mm(bl, high) + mm(bh, rest)

    scale = 1.0 / math.sqrt(PHASES * quarter)
    grad_long = [swap(x) for x in grad_long] + grad_long
    grads = []
    for phase, at in enumerate(starts):
        x = lane_tile(times, phase)
        grads.append(jnp.where(low, x * scale, x + gain * grad_long[phase]))
        send_ref[:, at : at + share, :] = grads[-1].astype(BF16).reshape(blocks, share, LANES)
    stage.give(0, 0)
    query_head = first * gather_first([saved_ref[8], saved_ref[9]], share)
    pair_head = both(gather_first(grads[:2], share))[1] * swap(pairs)
    heads = []
    for x in (query_head, pair_head):
        heads.append(jnp.concatenate([x[8:], jnp.zeros((8, LANES), F32)], axis=0))
    send_ref[:, rows:, :] = exact_groups(*heads)


def unpacked(ref, at, half, order):
    tiles = []
    for tile in range(ref.shape[0] // 2):
        x, y = [ref[2 * tile + i, at : at + half].astype(F32) for i in range(2)]
        top, bottom = pair(x, y)
        tiles.append(jnp.concatenate([top, bottom], axis=0))
    return mm(order, jnp.concatenate(tiles, axis=1).astype(BF16))


def pair_strip_of(ref, at):
    sides = [[], []]
    for tile in range(ref.shape[0] // 2):
        x, y = [ref[2 * tile + i, at : at + STRIP].astype(F32)[8:] for i in range(2)]
        for side, z in zip(sides, pair(x, y)):
            side.append(z)
    return [columns(side) for side in sides]


def gate_kernel(stage):
    recv_ref, gated_ref, grad_ref, tops_ref = stage.take(0), *[stage.out(i) for i in range(3)]
    rows = recv_ref.shape[1] - STRIP
    key, value = [x[0:2] + x[2:4] for x in pair_strip_of(recv_ref, rows)]
    tops_ref[...] = jnp.concatenate([key, value, key, value], axis=0)
    long_out = unpacked(recv_ref, 0, rows // 2, row_order(rows, back=True))
    query = stage.take(1)[0]
    grad_ref[...] = stage.take(2)[...] * long_out
    stage.give(1)
    gated_ref[...] = (query * long_out).astype(BF16)
    strip = strip_of(recv_ref, rows)
    first = strip + earlier(strip, 2)
    row = lax.broadcasted_iota(jnp.int32, first.shape, 0)
    first = jnp.where(row < 2, first, query[:STRIP])
    gated_ref[:STRIP, :] = (first * long_out[:STRIP]).astype(BF16)


def output_kernel(parts, stage):
    w_ref, total = stage.take(0), None
    for part in range(parts):
        gated = stage.take(1 + part)[...]
        width = gated.shape[1]
        term = mm(gated, w_ref[part * width : (part + 1) * width, :])
        total = term if total is None else total + term
    stage.out(0)[...] = total.astype(BF16)


def end_kernel(stage):
    recv_ref, grad_ref, filter_ref = stage.take(0), stage.out(0), stage.out(1)
    rows = filter_ref.shape[0]
    order = row_order(rows, back=True)
    sides = [[], []]
    for tile in range(recv_ref.shape[0] // 2):
        x, y = [recv_ref[2 * tile + i, :rows].astype(F32) for i in range(2)]
        for side, z in zip(sides, pair(x, y)):
            side.append(z.astype(BF16))
    taps, mixed = [mm(order, columns(side)) for side in sides]
    filter_ref[...] = taps
    stage.give(1)
    weight_ref, tops, short_ref = stage.take(1), stage.take(2)[...], stage.take(3)
    row = lax.broadcasted_iota(jnp.int32, mixed.shape, 0)
    heads = [x[0:2] + x[2:4] for x in pair_strip_of(recv_ref, rows)]
    for i in range(2):
        top = tops[2 - 2 * i : 4 - 2 * i]
        other = jnp.where(row == 0, top[0:1], jnp.where(row == 1, top[1:2], short_ref[1 - i]))
        grad_ref[i] = adjoint_of(mixed * other, heads[i], weight_ref[1 + i]).astype(BF16)
    stage.give(0, 0)
    strip = strip_of(recv_ref, rows)
    head = strip[0:2] + strip[2:4]
    grad_ref[2] = adjoint_of(stage.take(4)[...], head, weight_ref[0]).astype(BF16)


def partner(x, axis, mask):
    return lax.ppermute(x, axis, [(i, i ^ mask) for i in range(lax.axis_size(axis))])


def exchanged(x, axis):
    return lax.all_to_all(x, axis, split_axis=0, concat_axis=0, tiled=True)


def owner_layer(qkv, filt, skip_gain, short_weight, w_out, g_out):
    shape = jax.ShapeDtypeStruct
    seq_parts, ch_parts = lax.axis_size("seq"), lax.axis_size("ch")
    rows, width = qkv.shape[1], qkv.shape[2]
    tokens = seq_parts * rows
    quarter = tokens // PHASES
    tables = jnp.asarray(phase_tables(tokens))
    table_flops = 2 * 2 * 2 * 3 * tokens * tokens // PHASES * LANES
    product_flops = 2 * rows * width * width * ch_parts
    half = rows // 2
    wide = shape((seq_parts, rows + STRIP, LANES), BF16)
    column = shape((rows, width), BF16)
    saved = shape((11, quarter, LANES), F32)
    gain = skip_gain[None, :]

    (send,) = call(start_kernel, [Far(wide)], Far(short_weight), Far(qkv), Far(filt))
    recv = exchanged(send, "seq")
    half_sums, w_kept, g_kept = call(
        first_product_kernel,
        [
            Near(shape((2, rows, width), BF16), kept=True),
            Near(w_out, kept=True),
            Near(g_out, kept=True),
        ],
        Far(g_out, into=2),
        Far(w_out, turned=(1, 3, 2, 0), into=1),
        flops=product_flops // 2,
    )
    half_sums = partner(half_sums, "ch", 1)
    across, own = call(
        second_product_kernel,
        [Near(column, kept=True), Near(shape((rows, width), F32), kept=True)],
        Near(g_kept),
        Near(w_kept),
        Near(half_sums),
        flops=product_flops // 2,
    )
    across = partner(across, "ch", 2)
    def pinned(x):
        return Near(x, kept=True)

    tables_back = Far(tables, [(2, 2)])
    exact = shape((rows, width), F32)
    tables_on, weight, gain, query, short = call(
        query_kernel,
        [
            pinned(shape((3, *tables.shape[1:]), BF16)),
            pinned(short_weight),
            pinned(gain),
            pinned(exact),
            Far(shape((3, rows, width), F32)),
        ],
        Far(qkv),
        Far(short_weight, into=1),
        Far(tables, [(0, 2), (4, 1)], into=0),
        Far(gain, into=2),
    )
    grad_long, grad_far = call(
        sum_kernel,
        [Far(shape((seq_parts, half + STRIP, LANES), BF16)), Far(exact)],
        Near(own),
        Near(across),
        Near(query),
    )
    send, saved = call(
        forward_kernel,
        [
            Far(wide, [(0, half), (half, half + STRIP)], axis=1),
            pinned(saved),
        ],
        pinned(recv),
        Near(weight),
        Near(gain),
        Near(tables_on),
        tables_back,
        Far(grad_long),
        flops=table_flops,
    )
    swapped = exchanged(send, "seq")
    (send,) = call(
        backward_kernel,
        [Far(wide, [(0, rows), (rows, STRIP)], axis=1)],
        Near(swapped),
        Near(saved),
        Near(tables_on),
        tables_back,
        flops=table_flops,
    )
    grad_recv = exchanged(send, "seq")
    gated, grad_query, tops = call(
        gate_kernel,
        [pinned(column), Far(exact), Far(shape((8, width), F32))],
        Near(swapped),
        Far(short, [(0, 1)]),
        Far(grad_far),
    )
    across = partner(gated, "ch", 2)
    near, far = partner(gated, "ch", 1), partner(across, "ch", 1)
    (output,) = call(
        functools.partial(output_kernel, ch_parts),
        [Far(column)],
        Near(w_kept),
        Near(gated),
        Near(near),
        Near(across),
        Near(far),
        flops=product_flops,
    )
    grad_qkv, grad_filter = call(
        end_kernel,
        [Far(shape((3, rows, width), BF16), [(1, 2), (0, 1)]), Far(exact)],
        Near(grad_recv),
        Far(short_weight),
        Far(tops),
        Far(short, [(1, 2)]),
        Far(grad_query),
    )
    return (output, grad_qkv, grad_filter)


def local(qkv, filt, skip_gain, short_weight, w_out, g_out):
    seq_parts = lax.axis_size("seq")
    rows, width = qkv.shape[1], qkv.shape[2]
    fits = width == HALF * seq_parts and rows % HALF == 0 and rows & (rows - 1) == 0 and rows * seq_parts <= 2048
    if fits and lax.axis_size("ch") == 4:
        return owner_layer(qkv, filt, skip_gain, short_weight, w_out, g_out)
    return spread_layer(qkv, filt, skip_gain, short_weight, w_out, g_out)


def solution(mesh):
    in_specs = (
        P(None, "seq", "ch"),
        P("seq", "ch"),
        P("ch"),
        P(None, None, "ch"),
        P(None, "ch"),
        P("seq", "ch"),
    )
    out_specs = (P("seq", "ch"), P(None, "seq", "ch"), P("seq", "ch"))
    return jax.shard_map(local, mesh=mesh, in_specs=in_specs, out_specs=out_specs, check_vma=False)
```

profile of v0, /device:TPU:0, one launch (start us, length us, event | category | flops | bytes accessed | tf_op | source)
XLA Modules:
  0.0 56.6 jit_solution(16937825269672941597)
XLA Ops:
  0.6 2.4 %shard_map.95 = bf16[8,144,128]{2,1,0:T(8,128)(2,1)} custom-call(f32[3,3,512]{2,1,0:T(4,128)} %refs_1_.7, bf16[3,128,512]{2,1,0:T(8,128)(2,1)} %refs_0_.5, f32[128,512]{1,0:T(8,128)} %refs_2_.2), custom_call_target="tpu_custom_call" | custom-call | bytes 968704 | tf_op jit(solution)/shard_map/pallas_call | solution.py:310
  3.0 7.3 %all-to-all-start = ((bf16[8,144,128]{2,1,0:T(8,128)(2,1)}), bf16[8,144,128]{2,1,0:T(8,128)(2,1)S(1)}, u32[]{:S(2)}, u32[]{:S(2)}) async-start(bf16[8,144,128]{2,1,0:T(8,128)(2,1)} %shard_map.95), calls=%async_computation | async-start | bytes 589824 | tf_op jit(solution)/shard_map/all_to_all | solution.py:802
  10.3 1.8 %shard_map.94 = (bf16[2,128,512]{2,1,0:T(8,128)(2,1)S(1)}, bf16[2048,512]{1,0:T(8,128)(2,1)S(1)}, bf16[128,512]{1,0:T(8,128)(2,1)S(1)}) custom-call(bf16[128,512]{1,0:T(8,128)(2,1)} %refs_0_.3, bf16[2048,512]{1,0:T(8,128)(2,1)} %refs_1_.4), custom_call_target="tpu_custom_call" | custom-call | flops 134217728 | bytes 4718592 | tf_op jit(solution)/shard_map/pallas_call | solution.py:310
  12.1 0.1 collective-permute-start
  12.2 1.5 %collective-permute-done.refs_2_ = bf16[2,128,512]{2,1,0:T(8,128)(2,1)S(1)} collective-permute-done((bf16[2,128,512]{2,1,0:T(8,128)(2,1)S(1)}, bf16[2,128,512]{2,1,0:T(8,128)(2,1)S(1)}, u32[]{:S(2)}, u32[]{:S(2)}) %collective-permute-start) | collective-permute-done | bytes 262176 | tf_op jit(solution)/shard_map/ppermute | solution.py:798
  13.7 0.5 shard_map.97
  14.2 1.6 %collective-permute-start.1 = (bf16[128,512]{1,0:T(8,128)(2,1)S(1)}, bf16[128,512]{1,0:T(8,128)(2,1)S(1)}, u32[]{:S(2)}, u32[]{:S(2)}) collective-permute-start(bf16[128,512]{1,0:T(8,128)(2,1)S(1)} %get-tuple-element.29), channel_id=1, source_target_pairs={{0,2},{1,3},{2,0},{3,1},{4,6},{5,7},{6,4},{7,5},{8,10},{9,11},{10,... | collective-permute-start | bytes 393224 | tf_op jit(solution)/shard_map/ppermute | solution.py:798
  15.8 2.4 %shard_map.96 = (bf16[3,256,512]{2,1,0:T(8,128)(2,1)S(1)}, f32[3,3,512]{2,1,0:T(4,128)S(1)}, f32[1,512]{1,0:T(1,128)S(1)}, f32[128,512]{1,0:T(8,128)S(1)}, f32[3,128,512]{2,1,0:T(8,128)}) custom-call(bf16[3,128,512]{2,1,0:T(8,128)(2,1)} %refs_0_.5, f32[3,3,512]{2,1,0:T(4,128)} %refs_1_.7, bf16[8,256,512]{2,1,0:T(8,128)(2,1)} %constant.2.clone.refs_2_.refs_4_.refs_3_, ...), custom_call_target="tpu_custom_call" | custom-call | bytes 4366336 | tf_op jit(solution)/shard_map/pallas_call | solution.py:310
  18.2 1.7 %collective-permute-done.1.refs_1_ = bf16[128,512]{1,0:T(8,128)(2,1)S(1)} collective-permute-done((bf16[128,512]{1,0:T(8,128)(2,1)S(1)}, bf16[128,512]{1,0:T(8,128)(2,1)S(1)}, u32[]{:S(2)}, u32[]{:S(2)}) %collective-permute-start.1) | collective-permute-done | bytes 131104 | tf_op jit(solution)/shard_map/ppermute | solution.py:798
  19.8 1.0 %shard_map.98 = (bf16[8,80,128]{2,1,0:T(8,128)(2,1)}, f32[128,512]{1,0:T(8,128)}) custom-call(f32[128,512]{1,0:T(8,128)S(1)} %get-tuple-element.28.refs_0_, bf16[128,512]{1,0:T(8,128)(2,1)S(1)} %collective-permute-done.1.refs_1_, f32[128,512]{1,0:T(8,128)S(1)} %get-tuple-element.30.refs_2_), custom_call_target="tpu_custom_call" | custom-call | bytes 1081344 | tf_op jit(solution)/shard_map/pallas_call | solution.py:310
  20.8 0.0 all-to-all-done.refs_0_
  20.8 2.5 %shard_map.99 = (bf16[8,144,128]{2,1,0:T(8,128)(2,1)}, f32[11,256,128]{2,1,0:T(8,128)S(1)}) custom-call(bf16[8,144,128]{2,1,0:T(8,128)(2,1)S(1)} %all-to-all-done.refs_0_, f32[3,3,512]{2,1,0:T(4,128)S(1)} %get-tuple-element.23.refs_1_, f32[1,512]{1,0:T(1,128)S(1)} %get-tuple-element.24.refs_2_, bf16[3,256,512]{2,1,0:T(8,128)(2,1)S(1)} %get-tuple-element.25.refs_3_.refs_2_, ...), custom_call_target="tpu_custom_call" | custom-call | flops 805306368 | bytes 5099520 | tf_op jit(solution)/shard_map/pallas_call | solution.py:310
  23.3 15.8 %all_to_all.15.refs_0_ = bf16[8,144,128]{2,1,0:T(8,128)(2,1)S(1)} all-to-all(bf16[8,144,128]{2,1,0:T(8,128)(2,1)} %get-tuple-element.32), channel_id=1, replica_groups=mesh['seq'=8,'ch'=4] {'seq'}, dimensions={0} | all-to-all | bytes 589824 | tf_op jit(solution)/shard_map/all_to_all | solution.py:802
  39.1 2.4 %shard_map.102 = bf16[8,144,128]{2,1,0:T(8,128)(2,1)} custom-call(bf16[8,144,128]{2,1,0:T(8,128)(2,1)S(1)} %all_to_all.15.refs_0_, f32[11,256,128]{2,1,0:T(8,128)S(1)} %get-tuple-element.36.refs_1_, bf16[3,256,512]{2,1,0:T(8,128)(2,1)S(1)} %get-tuple-element.25.refs_3_.refs_2_, bf16[8,256,512]{2,1,0:T(8,128)(2,1)} %constant.2.clone.refs_2_.refs_4_.refs_3_), custom_call_target="tpu_custom_call" | custom-call | flops 805306368 | bytes 4915200 | tf_op jit(solution)/shard_map/pallas_call | solution.py:310
  41.6 3.4 %all-to-all-start.2 = ((bf16[8,144,128]{2,1,0:T(8,128)(2,1)}), bf16[8,144,128]{2,1,0:T(8,128)(2,1)S(1)}, u32[]{:S(2)}, u32[]{:S(2)}) async-start(bf16[8,144,128]{2,1,0:T(8,128)(2,1)} %shard_map.102), calls=%async_computation.2 | async-start | bytes 589824 | tf_op jit(solution)/shard_map/all_to_all | solution.py:802
  45.0 1.8 %shard_map.100 = (bf16[128,512]{1,0:T(8,128)(2,1)S(1)}, f32[128,512]{1,0:T(8,128)}, f32[8,512]{1,0:T(8,128)}) custom-call(bf16[8,144,128]{2,1,0:T(8,128)(2,1)S(1)} %all_to_all.15.refs_0_, f32[3,128,512]{2,1,0:T(8,128)} %get-tuple-element.33.refs_1_.refs_3_, f32[128,512]{1,0:T(8,128)} %get-tuple-element.34.refs_2_), custom_call_target="tpu_custom_call" | custom-call | bytes 1753088 | tf_op jit(solution)/shard_map/pallas_call | solution.py:310
  46.8 1.6 %collective-permute-start.3 = (bf16[128,512]{1,0:T(8,128)(2,1)S(1)}, bf16[128,512]{1,0:T(8,128)(2,1)S(1)}, u32[]{:S(2)}, u32[]{:S(2)}) collective-permute-start(bf16[128,512]{1,0:T(8,128)(2,1)S(1)} %get-tuple-element.35.refs_1_), channel_id=1, source_target_pairs={{0,2},{1,3},{2,0},{3,1},{4,6},{5,7},{6,4},{7,5},{8,10},{9,11},{10,... | collective-permute-start | bytes 393224 | tf_op jit(solution)/shard_map/ppermute | solution.py:798
  48.4 0.0 collective-permute-start.2
  48.4 3.5 %collective-permute-done.3.refs_3_ = bf16[128,512]{1,0:T(8,128)(2,1)S(1)} collective-permute-done((bf16[128,512]{1,0:T(8,128)(2,1)S(1)}, bf16[128,512]{1,0:T(8,128)(2,1)S(1)}, u32[]{:S(2)}, u32[]{:S(2)}) %collective-permute-start.3) | collective-permute-done | bytes 131104 | tf_op jit(solution)/shard_map/ppermute | solution.py:798
  51.9 0.0 collective-permute-start.4
  51.9 0.0 collective-permute-done.2.refs_2_
  51.9 1.3 %collective-permute-done.4.refs_4_ = bf16[128,512]{1,0:T(8,128)(2,1)S(1)} collective-permute-done((bf16[128,512]{1,0:T(8,128)(2,1)S(1)}, bf16[128,512]{1,0:T(8,128)(2,1)S(1)}, u32[]{:S(2)}, u32[]{:S(2)}) %collective-permute-start.4) | collective-permute-done | bytes 131104 | tf_op jit(solution)/shard_map/ppermute | solution.py:798
  53.2 1.1 %shard_map.101 = bf16[128,512]{1,0:T(8,128)(2,1)} custom-call(bf16[2048,512]{1,0:T(8,128)(2,1)S(1)} %get-tuple-element.22.refs_1_.refs_0_, bf16[128,512]{1,0:T(8,128)(2,1)S(1)} %get-tuple-element.35.refs_1_, bf16[128,512]{1,0:T(8,128)(2,1)S(1)} %collective-permute-done.2.refs_2_, bf16[128,512]{1,0:T(8,128)(2,1)S(1)} %collective-permute-done.3.refs_3_, ...), custom_call_target="tpu_custom_call" | custom-call | flops 268435456 | bytes 2752512 | tf_op jit(solution)/shard_map/pallas_call | solution.py:310
  54.4 0.0 all-to-all-done.2.refs_0_
  54.4 2.2 %shard_map.103 = (bf16[3,128,512]{2,1,0:T(8,128)(2,1)}, f32[128,512]{1,0:T(8,128)}) custom-call(bf16[8,144,128]{2,1,0:T(8,128)(2,1)S(1)} %all-to-all-done.2.refs_0_, f32[3,3,512]{2,1,0:T(4,128)} %refs_1_.7, f32[8,512]{1,0:T(8,128)} %get-tuple-element.37.refs_2_, f32[3,128,512]{2,1,0:T(8,128)} %get-tuple-element.33.refs_1_.refs_3_, ...), custom_call_target="tpu_custom_call" | custom-call | bytes 2033664 | tf_op jit(solution)/shard_map/pallas_call | solution.py:310
Async XLA Ops:
  3.0 17.7 %all-to-all-start = ((bf16[8,144,128]{2,1,0:T(8,128)(2,1)}), bf16[8,144,128]{2,1,0:T(8,128)(2,1)S(1)}, u32[]{:S(2)}, u32[]{:S(2)}) async-start(bf16[8,144,128]{2,1,0:T(8,128)(2,1)} %shard_map.95), calls=%async_computation | async-start | bytes 589824 | tf_op jit(solution)/shard_map/all_to_all | solution.py:802
  12.1 1.6 %collective-permute-start = (bf16[2,128,512]{2,1,0:T(8,128)(2,1)S(1)}, bf16[2,128,512]{2,1,0:T(8,128)(2,1)S(1)}, u32[]{:S(2)}, u32[]{:S(2)}) collective-permute-start(bf16[2,128,512]{2,1,0:T(8,128)(2,1)S(1)} %get-tuple-element.27), channel_id=1, source_target_pairs={{0,1},{1,0},{2,3},{3,2},{4,5},{5,4},{6,7},{7,6},{8,9},{9,8},{10,11... | collective-permute-start | bytes 786440 | tf_op jit(solution)/shard_map/ppermute | solution.py:798
  14.2 5.6 %collective-permute-start.1 = (bf16[128,512]{1,0:T(8,128)(2,1)S(1)}, bf16[128,512]{1,0:T(8,128)(2,1)S(1)}, u32[]{:S(2)}, u32[]{:S(2)}) collective-permute-start(bf16[128,512]{1,0:T(8,128)(2,1)S(1)} %get-tuple-element.29), channel_id=1, source_target_pairs={{0,2},{1,3},{2,0},{3,1},{4,6},{5,7},{6,4},{7,5},{8,10},{9,11},{10,... | collective-permute-start | bytes 393224 | tf_op jit(solution)/shard_map/ppermute | solution.py:798
  41.6 12.8 %all-to-all-start.2 = ((bf16[8,144,128]{2,1,0:T(8,128)(2,1)}), bf16[8,144,128]{2,1,0:T(8,128)(2,1)S(1)}, u32[]{:S(2)}, u32[]{:S(2)}) async-start(bf16[8,144,128]{2,1,0:T(8,128)(2,1)} %shard_map.102), calls=%async_computation.2 | async-start | bytes 589824 | tf_op jit(solution)/shard_map/all_to_all | solution.py:802
  46.8 5.0 %collective-permute-start.3 = (bf16[128,512]{1,0:T(8,128)(2,1)S(1)}, bf16[128,512]{1,0:T(8,128)(2,1)S(1)}, u32[]{:S(2)}, u32[]{:S(2)}) collective-permute-start(bf16[128,512]{1,0:T(8,128)(2,1)S(1)} %get-tuple-element.35.refs_1_), channel_id=1, source_target_pairs={{0,2},{1,3},{2,0},{3,1},{4,6},{5,7},{6,4},{7,5},{8,10},{9,11},{10,... | collective-permute-start | bytes 393224 | tf_op jit(solution)/shard_map/ppermute | solution.py:798
  48.4 3.5 %collective-permute-start.2 = (bf16[128,512]{1,0:T(8,128)(2,1)S(1)}, bf16[128,512]{1,0:T(8,128)(2,1)S(1)}, u32[]{:S(2)}, u32[]{:S(2)}) collective-permute-start(bf16[128,512]{1,0:T(8,128)(2,1)S(1)} %get-tuple-element.35.refs_1_), channel_id=1, source_target_pairs={{0,1},{1,0},{2,3},{3,2},{4,5},{5,4},{6,7},{7,6},{8,9},{9,8},{10,11... | collective-permute-start | bytes 393224 | tf_op jit(solution)/shard_map/ppermute | solution.py:798
  51.9 1.3 %collective-permute-start.4 = (bf16[128,512]{1,0:T(8,128)(2,1)S(1)}, bf16[128,512]{1,0:T(8,128)(2,1)S(1)}, u32[]{:S(2)}, u32[]{:S(2)}) collective-permute-start(bf16[128,512]{1,0:T(8,128)(2,1)S(1)} %collective-permute-done.3.refs_3_), channel_id=1, source_target_pairs={{0,1},{1,0},{2,3},{3,2},{4,5},{5,4},{6,7},{7,6},{8,9},{9,8},{10,11... | collective-permute-start | bytes 393224 | tf_op jit(solution)/shard_map/ppermute | solution.py:798
where the time goes:
time: 57.1 us; the launch traced here: 56.6 us
  Pallas kernels  18.1 us (32%)
  blocking collectives  15.8 us (28%)
  starting transfers between devices  13.9 us (24%)
  waiting for transfers between devices  7.98 us (14%)
  between operations  0.74 us (1%)
    pallas_call x10, Pallas kernels, call(): pl.pallas_call(functools.partial(staged, kernel, items, len(args)), out_s...  18.1 us
    all_to_all x1, blocking collectives, exchanged(): return lax.all_to_all(x, axis, split_axis=0, concat_axis=0, tiled=True)  15.8 us
    all_to_all x2, starting transfers between devices, exchanged(): return lax.all_to_all(x, axis, split_axis=0, concat_axis=0, tiled=True)  10.7 us
    ppermute x5, waiting for transfers between devices, partner(): lax.ppermute(x, axis, [(i, i ^ mask) for i in range(lax.axis_size(axis))])  7.98 us
    ppermute x5, starting transfers between devices, partner(): lax.ppermute(x, axis, [(i, i ^ mask) for i in range(lax.axis_size(axis))])  3.21 us
  transfers between devices with their start and end apart: 7, of which 4 were waited for; matrix products, arithmetic and copies ran while one was open for 0% of the time, Pallas kernels for 15%

commit v1 on v0

--- a/solution.py
+++ b/solution.py
@@ -476,15 +476,15 @@
     stage.out(3)[...] = short_ref[0]
 
 
-def sum_kernel(stage):
-    send_ref, kept_ref = stage.out(0), stage.out(1)
-    grad_gated = stage.take(0)[...] + stage.take(1)[...].astype(F32)
-    kept_ref[...] = grad_gated
-    stage.give(1)
+def put_grads(stage, at, send_ref):
+    grad_gated = stage.take(at)[...] + stage.take(at + 1)[...].astype(F32)
+    stage.out(2)[...] = grad_gated
+    stage.give(2)
     rows = grad_gated.shape[0]
     first = exact_rows(grad_gated[:2])
-    put_strip(jnp.concatenate([jnp.zeros_like(first), first], axis=0), send_ref, rows // 2)
-    put_rows(mm(row_order(rows), (grad_gated * stage.take(2)[...]).astype(BF16)), send_ref, 0)
+    put_strip(jnp.concatenate([jnp.zeros_like(first), first], axis=0), send_ref, rows)
+    grad_long = (grad_gated * stage.take(at + 2)[...]).astype(BF16)
+    put_rows(mm(row_order(rows), grad_long), send_ref, rows // 2)
 
 
 def spread_phases(parts):
@@ -661,9 +661,8 @@
     both_parts = [jnp.where(wide, z, y - z).astype(BF16) for y, z in zip(values, wider)]
     high = [jnp.where(wide, wider[i], wider[i + 2]).astype(BF16) for i in range(2)]
     main, more = mm(bh, columns(both_parts)), mm(bl, columns(high))
-    grad_ref = stage.take(5)
-    send_ref[:, rows // 2 : rows, :] = grad_ref[:, : rows // 2, :]
-    send_ref[:, rows:, :] = strip + grad_ref[:, rows // 2 :, :]
+    put_grads(stage, 5, send_ref)
+    send_ref[:, rows:, :] = strip + send_ref[:, rows:, :]
     stage.give(0, 1)
     summed = [y + swap(y) for y in (lane_tile(main, phase) for phase in range(PHASES))]
     for i in range(2):
@@ -743,14 +742,14 @@
 
 
 def gate_kernel(stage):
-    recv_ref, gated_ref, grad_ref, tops_ref = stage.take(0), *[stage.out(i) for i in range(3)]
+    recv_ref, gated_ref, long_ref, tops_ref = stage.take(0), *[stage.out(i) for i in range(3)]
     rows = recv_ref.shape[1] - STRIP
     key, value = [x[0:2] + x[2:4] for x in pair_strip_of(recv_ref, rows)]
     tops_ref[...] = jnp.concatenate([key, value, key, value], axis=0)
     long_out = unpacked(recv_ref, 0, rows // 2, row_order(rows, back=True))
+    long_ref[...] = long_out
+    stage.give(1)
     query = stage.take(1)[0]
-    grad_ref[...] = stage.take(2)[...] * long_out
-    stage.give(1)
     gated_ref[...] = (query * long_out).astype(BF16)
     strip = strip_of(recv_ref, rows)
     first = strip + earlier(strip, 2)
@@ -791,7 +790,8 @@
     stage.give(0, 0)
     strip = strip_of(recv_ref, rows)
     head = strip[0:2] + strip[2:4]
-    grad_ref[2] = adjoint_of(stage.take(4)[...], head, weight_ref[0]).astype(BF16)
+    grad_query = stage.take(4)[...] * stage.take(5)[...]
+    grad_ref[2] = adjoint_of(grad_query, head, weight_ref[0]).astype(BF16)
 
 
 def partner(x, axis, mask):
@@ -859,25 +859,21 @@
         Far(tables, [(0, 2), (4, 1)], into=0),
         Far(gain, into=2),
     )
-    grad_long, grad_far = call(
-        sum_kernel,
-        [Far(shape((seq_parts, half + STRIP, LANES), BF16)), Far(exact)],
-        Near(own),
-        Near(across),
-        Near(query),
-    )
-    send, saved = call(
+    send, saved, grad_far = call(
         forward_kernel,
         [
             Far(wide, [(0, half), (half, half + STRIP)], axis=1),
             pinned(saved),
+            Far(exact),
         ],
         pinned(recv),
         Near(weight),
         Near(gain),
         Near(tables_on),
         tables_back,
-        Far(grad_long),
+        Near(own),
+        Near(across),
+        Near(query),
         flops=table_flops,
     )
     swapped = exchanged(send, "seq")
@@ -891,12 +887,11 @@
         flops=table_flops,
     )
     grad_recv = exchanged(send, "seq")
-    gated, grad_query, tops = call(
+    gated, long_out, tops = call(
         gate_kernel,
         [pinned(column), Far(exact), Far(shape((8, width), F32))],
         Near(swapped),
         Far(short, [(0, 1)]),
-        Far(grad_far),
     )
     across = partner(gated, "ch", 2)
     near, far = partner(gated, "ch", 1), partner(across, "ch", 1)
@@ -917,7 +912,8 @@
         Far(short_weight),
         Far(tops),
         Far(short, [(1, 2)]),
-        Far(grad_query),
+        Far(long_out),
+        Far(grad_far),
     )
     return (output, grad_qkv, grad_filter)
 

time: 57.1 us -> 58.4 us (1.023)
  local copies, waits for them, and re-layouts: 0 us -> 3.21 us
  Pallas kernels: 18.1 us -> 16.7 us
  waiting for transfers between devices: 7.98 us -> 7.31 us
    unnamed x0 -> x8, local copies, waits for them, and re-layouts: none -> 3.21 us
    pallas_call x10 -> x9, Pallas kernels: 18.1 us -> 16.7 us  [call(): pl.pallas_call(functools.partial(staged, kernel, items, len(args)), out_s...]
    ppermute x5, waiting for transfers between devices: 7.98 us -> 7.3 us  [partner(): lax.ppermute(x, axis, [(i, i ^ mask) for i in range(lax.axis_size(axis))])]
  transfers between devices with their start and end apart: 7 -> 7, of which waited for: 4 -> 4; matrix products, arithmetic and copies ran while one was open for 0% -> 0% of each run, Pallas kernels for 15% -> 13%
where the time goes in v1:
time: 58.4 us; the launch traced here: 57.7 us
  Pallas kernels  16.7 us (29%)
  blocking collectives  15.9 us (27%)
  starting transfers between devices  13.9 us (24%)
  waiting for transfers between devices  7.31 us (13%)
  local copies, waits for them, and re-layouts  3.21 us (5%)
  between operations  0.73 us (1%)
    pallas_call x9, Pallas kernels, call(): pl.pallas_call(functools.partial(staged, kernel, items, len(args)), out_s...  16.7 us
    all_to_all x1, blocking collectives, exchanged(): return lax.all_to_all(x, axis, split_axis=0, concat_axis=0, tiled=True)  15.9 us
    all_to_all x2, starting transfers between devices, exchanged(): return lax.all_to_all(x, axis, split_axis=0, concat_axis=0, tiled=True)  10.7 us
    ppermute x5, waiting for transfers between devices, partner(): lax.ppermute(x, axis, [(i, i ^ mask) for i in range(lax.axis_size(axis))])  7.3 us
    unnamed x8, local copies, waits for them, and re-layouts  3.21 us
    ppermute x5, starting transfers between devices, partner(): lax.ppermute(x, axis, [(i, i ^ mask) for i in range(lax.axis_size(axis))])  3.2 us
  transfers between devices with their start and end apart: 7, of which 4 were waited for; matrix products, arithmetic and copies ran while one was open for 0% of the time, Pallas kernels for 13%

profile of v1, /device:TPU:0, one launch (start us, length us, event | category | flops | bytes accessed | tf_op | source)
XLA Modules:
  0.0 57.7 jit_solution(9311467800351922669)
XLA Ops:
  0.6 2.4 %shard_map.95 = bf16[8,144,128]{2,1,0:T(8,128)(2,1)} custom-call(f32[3,3,512]{2,1,0:T(4,128)} %refs_1_.7, bf16[3,128,512]{2,1,0:T(8,128)(2,1)} %refs_0_.5, f32[128,512]{1,0:T(8,128)} %refs_2_.2), custom_call_target="tpu_custom_call" | custom-call | bytes 968704 | tf_op jit(solution)/shard_map/pallas_call | solution.py:310
  3.0 7.3 %all-to-all-start = ((bf16[8,144,128]{2,1,0:T(8,128)(2,1)}), bf16[8,144,128]{2,1,0:T(8,128)(2,1)S(1)}, u32[]{:S(2)}, u32[]{:S(2)}) async-start(bf16[8,144,128]{2,1,0:T(8,128)(2,1)} %shard_map.95), calls=%async_computation | async-start | bytes 589824 | tf_op jit(solution)/shard_map/all_to_all | solution.py:802
  10.3 1.8 %shard_map.94 = (bf16[2,128,512]{2,1,0:T(8,128)(2,1)S(1)}, bf16[2048,512]{1,0:T(8,128)(2,1)S(1)}, bf16[128,512]{1,0:T(8,128)(2,1)S(1)}) custom-call(bf16[128,512]{1,0:T(8,128)(2,1)} %refs_0_.3, bf16[2048,512]{1,0:T(8,128)(2,1)} %refs_1_.4), custom_call_target="tpu_custom_call" | custom-call | flops 134217728 | bytes 4718592 | tf_op jit(solution)/shard_map/pallas_call | solution.py:310
  12.1 0.1 collective-permute-start
  12.2 1.5 %collective-permute-done.refs_2_ = bf16[2,128,512]{2,1,0:T(8,128)(2,1)S(1)} collective-permute-done((bf16[2,128,512]{2,1,0:T(8,128)(2,1)S(1)}, bf16[2,128,512]{2,1,0:T(8,128)(2,1)S(1)}, u32[]{:S(2)}, u32[]{:S(2)}) %collective-permute-start) | collective-permute-done | bytes 262176 | tf_op jit(solution)/shard_map/ppermute | solution.py:798
  13.7 0.5 shard_map.97
  14.2 1.6 %collective-permute-start.1 = (bf16[128,512]{1,0:T(8,128)(2,1)S(1)}, bf16[128,512]{1,0:T(8,128)(2,1)S(1)}, u32[]{:S(2)}, u32[]{:S(2)}) collective-permute-start(bf16[128,512]{1,0:T(8,128)(2,1)S(1)} %get-tuple-element.28), channel_id=1, source_target_pairs={{0,2},{1,3},{2,0},{3,1},{4,6},{5,7},{6,4},{7,5},{8,10},{9,11},{10,... | collective-permute-start | bytes 393224 | tf_op jit(solution)/shard_map/ppermute | solution.py:798
  15.8 2.4 %shard_map.96 = (bf16[3,256,512]{2,1,0:T(8,128)(2,1)S(1)}, f32[3,3,512]{2,1,0:T(4,128)S(1)}, f32[1,512]{1,0:T(1,128)S(1)}, f32[128,512]{1,0:T(8,128)S(1)}, f32[3,128,512]{2,1,0:T(8,128)}) custom-call(bf16[3,128,512]{2,1,0:T(8,128)(2,1)} %refs_0_.5, f32[3,3,512]{2,1,0:T(4,128)} %refs_1_.7, bf16[8,256,512]{2,1,0:T(8,128)(2,1)} %constant.2.clone.refs_2_.refs_4_.refs_3_, ...), custom_call_target="tpu_custom_call" | custom-call | bytes 4366336 | tf_op jit(solution)/shard_map/pallas_call | solution.py:310
  18.1 0.0 copy-start
  18.1 0.7 %copy-done = f32[128,512]{1,0:T(8,128)} copy-done((f32[128,512]{1,0:T(8,128)}, f32[128,512]{1,0:T(8,128)S(1)}, u32[]{:S(2)}) %copy-start) | copy-done | bytes 262168
  18.8 1.0 %collective-permute-done.1.refs_6_ = bf16[128,512]{1,0:T(8,128)(2,1)S(1)} collective-permute-done((bf16[128,512]{1,0:T(8,128)(2,1)S(1)}, bf16[128,512]{1,0:T(8,128)(2,1)S(1)}, u32[]{:S(2)}, u32[]{:S(2)}) %collective-permute-start.1) | collective-permute-done | bytes 131104 | tf_op jit(solution)/shard_map/ppermute | solution.py:798
  19.8 0.0 copy-start.2
  19.8 0.7 %copy-done.2 = bf16[128,512]{1,0:T(8,128)(2,1)} copy-done((bf16[128,512]{1,0:T(8,128)(2,1)}, bf16[128,512]{1,0:T(8,128)(2,1)S(1)}, u32[]{:S(2)}) %copy-start.2) | copy-done | bytes 131096
  20.5 0.0 all-to-all-done.refs_0_
  20.5 0.0 copy-start.1
  20.5 0.9 %copy-done.1 = f32[128,512]{1,0:T(8,128)S(1)} copy-done((f32[128,512]{1,0:T(8,128)S(1)}, f32[128,512]{1,0:T(8,128)}, u32[]{:S(2)}) %copy-start.1) | copy-done | bytes 262168
  21.4 0.0 copy-start.3
  21.4 0.9 %copy-done.3 = bf16[128,512]{1,0:T(8,128)(2,1)S(1)} copy-done((bf16[128,512]{1,0:T(8,128)(2,1)S(1)}, bf16[128,512]{1,0:T(8,128)(2,1)}, u32[]{:S(2)}) %copy-start.3) | copy-done | bytes 131096
  22.3 2.4 %shard_map.98 = (bf16[8,144,128]{2,1,0:T(8,128)(2,1)}, f32[11,256,128]{2,1,0:T(8,128)S(1)}, f32[128,512]{1,0:T(8,128)}) custom-call(bf16[8,144,128]{2,1,0:T(8,128)(2,1)S(1)} %all-to-all-done.refs_0_, f32[3,3,512]{2,1,0:T(4,128)S(1)} %get-tuple-element.22.refs_1_, f32[1,512]{1,0:T(1,128)S(1)} %get-tuple-element.23.refs_2_, ...), custom_call_target="tpu_custom_call" | custom-call | flops 805306368 | bytes 5853184 | tf_op jit(solution)/shard_map/pallas_call | solution.py:310
  24.7 15.9 %all_to_all.15.refs_0_ = bf16[8,144,128]{2,1,0:T(8,128)(2,1)S(1)} all-to-all(bf16[8,144,128]{2,1,0:T(8,128)(2,1)} %get-tuple-element.30), channel_id=1, replica_groups=mesh['seq'=8,'ch'=4] {'seq'}, dimensions={0} | all-to-all | bytes 589824 | tf_op jit(solution)/shard_map/all_to_all | solution.py:802
  40.6 2.4 %shard_map.101 = bf16[8,144,128]{2,1,0:T(8,128)(2,1)} custom-call(bf16[8,144,128]{2,1,0:T(8,128)(2,1)S(1)} %all_to_all.15.refs_0_, f32[11,256,128]{2,1,0:T(8,128)S(1)} %get-tuple-element.33.refs_1_, bf16[3,256,512]{2,1,0:T(8,128)(2,1)S(1)} %get-tuple-element.24.refs_3_.refs_2_, bf16[8,256,512]{2,1,0:T(8,128)(2,1)} %constant.2.clone.refs_2_.refs_4_.refs_3_), custom_call_target="tpu_custom_call" | custom-call | flops 805306368 | bytes 4915200 | tf_op jit(solution)/shard_map/pallas_call | solution.py:310
  43.0 3.4 %all-to-all-start.2 = ((bf16[8,144,128]{2,1,0:T(8,128)(2,1)}), bf16[8,144,128]{2,1,0:T(8,128)(2,1)S(1)}, u32[]{:S(2)}, u32[]{:S(2)}) async-start(bf16[8,144,128]{2,1,0:T(8,128)(2,1)} %shard_map.101), calls=%async_computation.2 | async-start | bytes 589824 | tf_op jit(solution)/shard_map/all_to_all | solution.py:802
  46.4 1.6 %shard_map.99 = (bf16[128,512]{1,0:T(8,128)(2,1)S(1)}, f32[128,512]{1,0:T(8,128)}, f32[8,512]{1,0:T(8,128)}) custom-call(bf16[8,144,128]{2,1,0:T(8,128)(2,1)S(1)} %all_to_all.15.refs_0_, f32[3,128,512]{2,1,0:T(8,128)} %get-tuple-element.31.refs_1_.refs_3_), custom_call_target="tpu_custom_call" | custom-call | bytes 1490944 | tf_op jit(solution)/shard_map/pallas_call | solution.py:310
  48.0 1.6 %collective-permute-start.3 = (bf16[128,512]{1,0:T(8,128)(2,1)S(1)}, bf16[128,512]{1,0:T(8,128)(2,1)S(1)}, u32[]{:S(2)}, u32[]{:S(2)}) collective-permute-start(bf16[128,512]{1,0:T(8,128)(2,1)S(1)} %get-tuple-element.32.refs_1_), channel_id=1, source_target_pairs={{0,2},{1,3},{2,0},{3,1},{4,6},{5,7},{6,4},{7,5},{8,10},{9,11},{10,... | collective-permute-start | bytes 393224 | tf_op jit(solution)/shard_map/ppermute | solution.py:798
  49.6 0.0 collective-permute-start.2
  49.6 3.5 %collective-permute-done.3.refs_3_ = bf16[128,512]{1,0:T(8,128)(2,1)S(1)} collective-permute-done((bf16[128,512]{1,0:T(8,128)(2,1)S(1)}, bf16[128,512]{1,0:T(8,128)(2,1)S(1)}, u32[]{:S(2)}, u32[]{:S(2)}) %collective-permute-start.3) | collective-permute-done | bytes 131104 | tf_op jit(solution)/shard_map/ppermute | solution.py:798
  53.0 0.0 collective-permute-start.4
  53.0 0.0 collective-permute-done.2.refs_2_
  53.0 1.3 %collective-permute-done.4.refs_4_ = bf16[128,512]{1,0:T(8,128)(2,1)S(1)} collective-permute-done((bf16[128,512]{1,0:T(8,128)(2,1)S(1)}, bf16[128,512]{1,0:T(8,128)(2,1)S(1)}, u32[]{:S(2)}, u32[]{:S(2)}) %collective-permute-start.4) | collective-permute-done | bytes 131104 | tf_op jit(solution)/shard_map/ppermute | solution.py:798
  54.4 1.1 %shard_map.100 = bf16[128,512]{1,0:T(8,128)(2,1)} custom-call(bf16[2048,512]{1,0:T(8,128)(2,1)S(1)} %get-tuple-element.21.refs_1_.refs_0_, bf16[128,512]{1,0:T(8,128)(2,1)S(1)} %get-tuple-element.32.refs_1_, bf16[128,512]{1,0:T(8,128)(2,1)S(1)} %collective-permute-done.2.refs_2_, bf16[128,512]{1,0:T(8,128)(2,1)S(1)} %collective-permute-done.3.refs_3_, ...), custom_call_target="tpu_custom_call" | custom-call | flops 268435456 | bytes 2752512 | tf_op jit(solution)/shard_map/pallas_call | solution.py:310
  55.5 0.0 all-to-all-done.2.refs_0_
  55.5 2.2 %shard_map.102 = (bf16[3,128,512]{2,1,0:T(8,128)(2,1)}, f32[128,512]{1,0:T(8,128)}) custom-call(bf16[8,144,128]{2,1,0:T(8,128)(2,1)S(1)} %all-to-all-done.2.refs_0_, f32[3,3,512]{2,1,0:T(4,128)} %refs_1_.7, f32[8,512]{1,0:T(8,128)} %get-tuple-element.34.refs_2_, f32[3,128,512]{2,1,0:T(8,128)} %get-tuple-element.31.refs_1_.refs_3_, ...), custom_call_target="tpu_custom_call" | custom-call | bytes 2295808 | tf_op jit(solution)/shard_map/pallas_call | solution.py:310
Async XLA Ops:
  3.0 17.4 %all-to-all-start = ((bf16[8,144,128]{2,1,0:T(8,128)(2,1)}), bf16[8,144,128]{2,1,0:T(8,128)(2,1)S(1)}, u32[]{:S(2)}, u32[]{:S(2)}) async-start(bf16[8,144,128]{2,1,0:T(8,128)(2,1)} %shard_map.95), calls=%async_computation | async-start | bytes 589824 | tf_op jit(solution)/shard_map/all_to_all | solution.py:802
  12.1 1.6 %collective-permute-start = (bf16[2,128,512]{2,1,0:T(8,128)(2,1)S(1)}, bf16[2,128,512]{2,1,0:T(8,128)(2,1)S(1)}, u32[]{:S(2)}, u32[]{:S(2)}) collective-permute-start(bf16[2,128,512]{2,1,0:T(8,128)(2,1)S(1)} %get-tuple-element.26), channel_id=1, source_target_pairs={{0,1},{1,0},{2,3},{3,2},{4,5},{5,4},{6,7},{7,6},{8,9},{9,8},{10,11... | collective-permute-start | bytes 786440 | tf_op jit(solution)/shard_map/ppermute | solution.py:798
  14.2 5.6 %collective-permute-start.1 = (bf16[128,512]{1,0:T(8,128)(2,1)S(1)}, bf16[128,512]{1,0:T(8,128)(2,1)S(1)}, u32[]{:S(2)}, u32[]{:S(2)}) collective-permute-start(bf16[128,512]{1,0:T(8,128)(2,1)S(1)} %get-tuple-element.28), channel_id=1, source_target_pairs={{0,2},{1,3},{2,0},{3,1},{4,6},{5,7},{6,4},{7,5},{8,10},{9,11},{10,... | collective-permute-start | bytes 393224 | tf_op jit(solution)/shard_map/ppermute | solution.py:798
  18.1 0.7 %copy-start = (f32[128,512]{1,0:T(8,128)}, f32[128,512]{1,0:T(8,128)S(1)}, u32[]{:S(2)}) copy-start(f32[128,512]{1,0:T(8,128)S(1)} %get-tuple-element.29.refs_7_) | copy-start | bytes 786436
  19.8 0.7 %copy-start.2 = (bf16[128,512]{1,0:T(8,128)(2,1)}, bf16[128,512]{1,0:T(8,128)(2,1)S(1)}, u32[]{:S(2)}) copy-start(bf16[128,512]{1,0:T(8,128)(2,1)S(1)} %collective-permute-done.1.refs_6_) | copy-start | bytes 393220
  20.5 1.0 %copy-start.1 = (f32[128,512]{1,0:T(8,128)S(1)}, f32[128,512]{1,0:T(8,128)}, u32[]{:S(2)}) copy-start(f32[128,512]{1,0:T(8,128)} %copy-done) | copy-start | bytes 786436
  21.4 0.9 %copy-start.3 = (bf16[128,512]{1,0:T(8,128)(2,1)S(1)}, bf16[128,512]{1,0:T(8,128)(2,1)}, u32[]{:S(2)}) copy-start(bf16[128,512]{1,0:T(8,128)(2,1)} %copy-done.2) | copy-start | bytes 393220
  43.0 12.5 %all-to-all-start.2 = ((bf16[8,144,128]{2,1,0:T(8,128)(2,1)}), bf16[8,144,128]{2,1,0:T(8,128)(2,1)S(1)}, u32[]{:S(2)}, u32[]{:S(2)}) async-start(bf16[8,144,128]{2,1,0:T(8,128)(2,1)} %shard_map.101), calls=%async_computation.2 | async-start | bytes 589824 | tf_op jit(solution)/shard_map/all_to_all | solution.py:802
  48.0 5.0 %collective-permute-start.3 = (bf16[128,512]{1,0:T(8,128)(2,1)S(1)}, bf16[128,512]{1,0:T(8,128)(2,1)S(1)}, u32[]{:S(2)}, u32[]{:S(2)}) collective-permute-start(bf16[128,512]{1,0:T(8,128)(2,1)S(1)} %get-tuple-element.32.refs_1_), channel_id=1, source_target_pairs={{0,2},{1,3},{2,0},{3,1},{4,6},{5,7},{6,4},{7,5},{8,10},{9,11},{10,... | collective-permute-start | bytes 393224 | tf_op jit(solution)/shard_map/ppermute | solution.py:798
  49.6 3.5 %collective-permute-start.2 = (bf16[128,512]{1,0:T(8,128)(2,1)S(1)}, bf16[128,512]{1,0:T(8,128)(2,1)S(1)}, u32[]{:S(2)}, u32[]{:S(2)}) collective-permute-start(bf16[128,512]{1,0:T(8,128)(2,1)S(1)} %get-tuple-element.32.refs_1_), channel_id=1, source_target_pairs={{0,1},{1,0},{2,3},{3,2},{4,5},{5,4},{6,7},{7,6},{8,9},{9,8},{10,11... | collective-permute-start | bytes 393224 | tf_op jit(solution)/shard_map/ppermute | solution.py:798
  53.0 1.3 %collective-permute-start.4 = (bf16[128,512]{1,0:T(8,128)(2,1)S(1)}, bf16[128,512]{1,0:T(8,128)(2,1)S(1)}, u32[]{:S(2)}, u32[]{:S(2)}) collective-permute-start(bf16[128,512]{1,0:T(8,128)(2,1)S(1)} %collective-permute-done.3.refs_3_), channel_id=1, source_target_pairs={{0,1},{1,0},{2,3},{3,2},{4,5},{5,4},{6,7},{7,6},{8,9},{9,8},{10,11... | collective-permute-start | bytes 393224 | tf_op jit(solution)/shard_map/ppermute | solution.py:798

commit v2 on v0

--- a/solution.py
+++ b/solution.py
@@ -697,6 +697,9 @@
     high, rest = halves(columns(grad_long))
     three = zip(two_sides(fh, high), two_sides(fl, high), two_sides(fh, rest))
     main = [x + y + z for x, y, z in three]
+    gate(grad_ref, stage.take(4)[0], *[stage.out(i) for i in (1, 2, 3)])
+    stage.give(2)
+    stage.give(3)
     sides = []
     for phase in range(PHASES):
         sides.append([both(lane_tile(x, phase % 2))[phase // 2] for x in main])
@@ -742,15 +745,12 @@
     return [columns(side) for side in sides]
 
 
-def gate_kernel(stage):
-    recv_ref, gated_ref, grad_ref, tops_ref = stage.take(0), *[stage.out(i) for i in range(3)]
+def gate(recv_ref, query, gated_ref, long_ref, tops_ref):
     rows = recv_ref.shape[1] - STRIP
     key, value = [x[0:2] + x[2:4] for x in pair_strip_of(recv_ref, rows)]
     tops_ref[...] = jnp.concatenate([key, value, key, value], axis=0)
     long_out = unpacked(recv_ref, 0, rows // 2, row_order(rows, back=True))
-    query = stage.take(1)[0]
-    grad_ref[...] = stage.take(2)[...] * long_out
-    stage.give(1)
+    long_ref[...] = long_out
     gated_ref[...] = (query * long_out).astype(BF16)
     strip = strip_of(recv_ref, rows)
     first = strip + earlier(strip, 2)
@@ -791,7 +791,8 @@
     stage.give(0, 0)
     strip = strip_of(recv_ref, rows)
     head = strip[0:2] + strip[2:4]
-    grad_ref[2] = adjoint_of(stage.take(4)[...], head, weight_ref[0]).astype(BF16)
+    grad_query = stage.take(4)[...] * stage.take(5)[...]
+    grad_ref[2] = adjoint_of(grad_query, head, weight_ref[0]).astype(BF16)
 
 
 def partner(x, axis, mask):
@@ -881,23 +882,22 @@
         flops=table_flops,
     )
     swapped = exchanged(send, "seq")
-    (send,) = call(
+    send, gated, long_out, tops = call(
         backward_kernel,
-        [Far(wide, [(0, rows), (rows, STRIP)], axis=1)],
+        [
+            Far(wide, [(0, rows), (rows, STRIP)], axis=1),
+            pinned(column),
+            Far(exact),
+            Far(shape((8, width), F32)),
+        ],
         Near(swapped),
         Near(saved),
         Near(tables_on),
         tables_back,
+        Far(short, [(0, 1)]),
         flops=table_flops,
     )
     grad_recv = exchanged(send, "seq")
-    gated, grad_query, tops = call(
-        gate_kernel,
-        [pinned(column), Far(exact), Far(shape((8, width), F32))],
-        Near(swapped),
-        Far(short, [(0, 1)]),
-        Far(grad_far),
-    )
     across = partner(gated, "ch", 2)
     near, far = partner(gated, "ch", 1), partner(across, "ch", 1)
     (output,) = call(
@@ -917,7 +917,8 @@
         Far(short_weight),
         Far(tops),
         Far(short, [(1, 2)]),
-        Far(grad_query),
+        Far(long_out),
+        Far(grad_far),
     )
     return (output, grad_qkv, grad_filter)
 

time: 57.1 us -> 57.6 us (level)
  waiting for transfers between devices: 7.98 us -> 9.1 us
  Pallas kernels: 18.1 us -> 17.5 us
    all_to_all x2, waiting for transfers between devices: 0.01 us -> 1.1 us  [exchanged(): return lax.all_to_all(x, axis, split_axis=0, concat_axis=0, tiled=True)]
    pallas_call x10 -> x9, Pallas kernels: 18.1 us -> 17.5 us  [call(): pl.pallas_call(functools.partial(staged, kernel, items, len(args)), out_s...]
  transfers between devices with their start and end apart: 7 -> 7, of which waited for: 4 -> 5; matrix products, arithmetic and copies ran while one was open for 0% -> 0% of each run, Pallas kernels for 15% -> 12%
where the time goes in v2:
time: 57.6 us; the launch traced here: 57.1 us
  Pallas kernels  17.5 us (30%)
  blocking collectives  15.9 us (28%)
  starting transfers between devices  13.9 us (24%)
  waiting for transfers between devices  9.1 us (16%)
  between operations  0.72 us (1%)
    pallas_call x9, Pallas kernels, call(): pl.pallas_call(functools.partial(staged, kernel, items, len(args)), out_s...  17.5 us
    all_to_all x1, blocking collectives, exchanged(): return lax.all_to_all(x, axis, split_axis=0, concat_axis=0, tiled=True)  15.9 us
    all_to_all x2, starting transfers between devices, exchanged(): return lax.all_to_all(x, axis, split_axis=0, concat_axis=0, tiled=True)  10.7 us
    ppermute x5, waiting for transfers between devices, partner(): lax.ppermute(x, axis, [(i, i ^ mask) for i in range(lax.axis_size(axis))])  7.99 us
    ppermute x5, starting transfers between devices, partner(): lax.ppermute(x, axis, [(i, i ^ mask) for i in range(lax.axis_size(axis))])  3.2 us
  transfers between devices with their start and end apart: 7, of which 5 were waited for; matrix products, arithmetic and copies ran while one was open for 0% of the time, Pallas kernels for 12%

profile of v2, /device:TPU:0, one launch (start us, length us, event | category | flops | bytes accessed | tf_op | source)
XLA Modules:
  0.0 57.1 jit_solution(15736496605060476153)
XLA Ops:
  0.6 2.4 %shard_map.95 = bf16[8,144,128]{2,1,0:T(8,128)(2,1)} custom-call(f32[3,3,512]{2,1,0:T(4,128)} %refs_1_.7, bf16[3,128,512]{2,1,0:T(8,128)(2,1)} %refs_0_.5, f32[128,512]{1,0:T(8,128)} %refs_2_.2), custom_call_target="tpu_custom_call" | custom-call | bytes 968704 | tf_op jit(solution)/shard_map/pallas_call | solution.py:310
  3.0 7.3 %all-to-all-start = ((bf16[8,144,128]{2,1,0:T(8,128)(2,1)}), bf16[8,144,128]{2,1,0:T(8,128)(2,1)S(1)}, u32[]{:S(2)}, u32[]{:S(2)}) async-start(bf16[8,144,128]{2,1,0:T(8,128)(2,1)} %shard_map.95), calls=%async_computation | async-start | bytes 589824 | tf_op jit(solution)/shard_map/all_to_all | solution.py:803
  10.3 1.8 %shard_map.94 = (bf16[2,128,512]{2,1,0:T(8,128)(2,1)S(1)}, bf16[2048,512]{1,0:T(8,128)(2,1)S(1)}, bf16[128,512]{1,0:T(8,128)(2,1)S(1)}) custom-call(bf16[128,512]{1,0:T(8,128)(2,1)} %refs_0_.3, bf16[2048,512]{1,0:T(8,128)(2,1)} %refs_1_.4), custom_call_target="tpu_custom_call" | custom-call | flops 134217728 | bytes 4718592 | tf_op jit(solution)/shard_map/pallas_call | solution.py:310
  12.1 0.1 collective-permute-start
  12.2 1.5 %collective-permute-done.refs_2_ = bf16[2,128,512]{2,1,0:T(8,128)(2,1)S(1)} collective-permute-done((bf16[2,128,512]{2,1,0:T(8,128)(2,1)S(1)}, bf16[2,128,512]{2,1,0:T(8,128)(2,1)S(1)}, u32[]{:S(2)}, u32[]{:S(2)}) %collective-permute-start) | collective-permute-done | bytes 262176 | tf_op jit(solution)/shard_map/ppermute | solution.py:799
  13.7 0.5 shard_map.97
  14.2 1.6 %collective-permute-start.1 = (bf16[128,512]{1,0:T(8,128)(2,1)S(1)}, bf16[128,512]{1,0:T(8,128)(2,1)S(1)}, u32[]{:S(2)}, u32[]{:S(2)}) collective-permute-start(bf16[128,512]{1,0:T(8,128)(2,1)S(1)} %get-tuple-element.30), channel_id=1, source_target_pairs={{0,2},{1,3},{2,0},{3,1},{4,6},{5,7},{6,4},{7,5},{8,10},{9,11},{10,... | collective-permute-start | bytes 393224 | tf_op jit(solution)/shard_map/ppermute | solution.py:799
  15.8 2.4 %shard_map.96 = (bf16[3,256,512]{2,1,0:T(8,128)(2,1)S(1)}, f32[3,3,512]{2,1,0:T(4,128)S(1)}, f32[1,512]{1,0:T(1,128)S(1)}, f32[128,512]{1,0:T(8,128)S(1)}, f32[3,128,512]{2,1,0:T(8,128)}) custom-call(bf16[3,128,512]{2,1,0:T(8,128)(2,1)} %refs_0_.5, f32[3,3,512]{2,1,0:T(4,128)} %refs_1_.7, bf16[8,256,512]{2,1,0:T(8,128)(2,1)} %constant.2.clone.refs_2_.refs_4_.refs_3_, ...), custom_call_target="tpu_custom_call" | custom-call | bytes 4366336 | tf_op jit(solution)/shard_map/pallas_call | solution.py:310
  18.2 1.7 %collective-permute-done.1.refs_1_ = bf16[128,512]{1,0:T(8,128)(2,1)S(1)} collective-permute-done((bf16[128,512]{1,0:T(8,128)(2,1)S(1)}, bf16[128,512]{1,0:T(8,128)(2,1)S(1)}, u32[]{:S(2)}, u32[]{:S(2)}) %collective-permute-start.1) | collective-permute-done | bytes 131104 | tf_op jit(solution)/shard_map/ppermute | solution.py:799
  19.8 1.0 %shard_map.98 = (bf16[8,80,128]{2,1,0:T(8,128)(2,1)}, f32[128,512]{1,0:T(8,128)}) custom-call(f32[128,512]{1,0:T(8,128)S(1)} %get-tuple-element.29.refs_0_, bf16[128,512]{1,0:T(8,128)(2,1)S(1)} %collective-permute-done.1.refs_1_, f32[128,512]{1,0:T(8,128)S(1)} %get-tuple-element.31.refs_2_), custom_call_target="tpu_custom_call" | custom-call | bytes 1081344 | tf_op jit(solution)/shard_map/pallas_call | solution.py:310
  20.8 0.0 all-to-all-done.refs_0_
  20.8 2.5 %shard_map.99 = (bf16[8,144,128]{2,1,0:T(8,128)(2,1)}, f32[11,256,128]{2,1,0:T(8,128)S(1)}) custom-call(bf16[8,144,128]{2,1,0:T(8,128)(2,1)S(1)} %all-to-all-done.refs_0_, f32[3,3,512]{2,1,0:T(4,128)S(1)} %get-tuple-element.24.refs_1_, f32[1,512]{1,0:T(1,128)S(1)} %get-tuple-element.25.refs_2_, bf16[3,256,512]{2,1,0:T(8,128)(2,1)S(1)} %get-tuple-element.26.refs_3_.refs_2_, ...), custom_call_target="tpu_custom_call" | custom-call | flops 805306368 | bytes 5099520 | tf_op jit(solution)/shard_map/pallas_call | solution.py:310
  23.3 15.9 %all_to_all.15.refs_0_ = bf16[8,144,128]{2,1,0:T(8,128)(2,1)S(1)} all-to-all(bf16[8,144,128]{2,1,0:T(8,128)(2,1)} %get-tuple-element.33), channel_id=1, replica_groups=mesh['seq'=8,'ch'=4] {'seq'}, dimensions={0} | all-to-all | bytes 589824 | tf_op jit(solution)/shard_map/all_to_all | solution.py:803
  39.1 3.7 %shard_map.100 = (bf16[8,144,128]{2,1,0:T(8,128)(2,1)}, bf16[128,512]{1,0:T(8,128)(2,1)S(1)}, f32[128,512]{1,0:T(8,128)}, f32[8,512]{1,0:T(8,128)}) custom-call(bf16[8,144,128]{2,1,0:T(8,128)(2,1)S(1)} %all_to_all.15.refs_0_, f32[11,256,128]{2,1,0:T(8,128)S(1)} %get-tuple-element.34.refs_1_, bf16[3,256,512]{2,1,0:T(8,128)(2,1)S(1)} %get-tuple-element.26.refs_3_.refs_2_, ...), custom_call_target="tpu_custom_call" | custom-call | flops 805306368 | bytes 6111232 | tf_op jit(solution)/shard_map/pallas_call | solution.py:310
  42.8 3.4 %all-to-all-start.2 = ((bf16[8,144,128]{2,1,0:T(8,128)(2,1)}), bf16[8,144,128]{2,1,0:T(8,128)(2,1)S(1)}, u32[]{:S(2)}, u32[]{:S(2)}) async-start(bf16[8,144,128]{2,1,0:T(8,128)(2,1)} %get-tuple-element.37), calls=%async_computation.2 | async-start | bytes 589824 | tf_op jit(solution)/shard_map/all_to_all | solution.py:803
  46.3 1.6 %collective-permute-start.3 = (bf16[128,512]{1,0:T(8,128)(2,1)S(1)}, bf16[128,512]{1,0:T(8,128)(2,1)S(1)}, u32[]{:S(2)}, u32[]{:S(2)}) collective-permute-start(bf16[128,512]{1,0:T(8,128)(2,1)S(1)} %get-tuple-element.36.refs_1_), channel_id=1, source_target_pairs={{0,2},{1,3},{2,0},{3,1},{4,6},{5,7},{6,4},{7,5},{8,10},{9,11},{10,... | collective-permute-start | bytes 393224 | tf_op jit(solution)/shard_map/ppermute | solution.py:799
  47.8 0.0 collective-permute-start.2
  47.8 3.5 %collective-permute-done.3.refs_3_ = bf16[128,512]{1,0:T(8,128)(2,1)S(1)} collective-permute-done((bf16[128,512]{1,0:T(8,128)(2,1)S(1)}, bf16[128,512]{1,0:T(8,128)(2,1)S(1)}, u32[]{:S(2)}, u32[]{:S(2)}) %collective-permute-start.3) | collective-permute-done | bytes 131104 | tf_op jit(solution)/shard_map/ppermute | solution.py:799
  51.3 0.0 collective-permute-start.4
  51.3 0.0 collective-permute-done.2.refs_2_
  51.3 1.3 %collective-permute-done.4.refs_4_ = bf16[128,512]{1,0:T(8,128)(2,1)S(1)} collective-permute-done((bf16[128,512]{1,0:T(8,128)(2,1)S(1)}, bf16[128,512]{1,0:T(8,128)(2,1)S(1)}, u32[]{:S(2)}, u32[]{:S(2)}) %collective-permute-start.4) | collective-permute-done | bytes 131104 | tf_op jit(solution)/shard_map/ppermute | solution.py:799
  52.7 1.1 %shard_map.101 = bf16[128,512]{1,0:T(8,128)(2,1)} custom-call(bf16[2048,512]{1,0:T(8,128)(2,1)S(1)} %get-tuple-element.23.refs_1_.refs_0_, bf16[128,512]{1,0:T(8,128)(2,1)S(1)} %get-tuple-element.36.refs_1_, bf16[128,512]{1,0:T(8,128)(2,1)S(1)} %collective-permute-done.2.refs_2_, bf16[128,512]{1,0:T(8,128)(2,1)S(1)} %collective-permute-done.3.refs_3_, ...), custom_call_target="tpu_custom_call" | custom-call | flops 268435456 | bytes 2752512 | tf_op jit(solution)/shard_map/pallas_call | solution.py:310
  53.8 1.1 %all-to-all-done.2.refs_0_ = bf16[8,144,128]{2,1,0:T(8,128)(2,1)S(1)} async-done(((bf16[8,144,128]{2,1,0:T(8,128)(2,1)}), bf16[8,144,128]{2,1,0:T(8,128)(2,1)S(1)}, u32[]{:S(2)}, u32[]{:S(2)}) %all-to-all-start.2) | async-done | bytes 294944 | tf_op jit(solution)/shard_map/all_to_all | solution.py:803
  54.9 2.2 %shard_map.102 = (bf16[3,128,512]{2,1,0:T(8,128)(2,1)}, f32[128,512]{1,0:T(8,128)}) custom-call(bf16[8,144,128]{2,1,0:T(8,128)(2,1)S(1)} %all-to-all-done.2.refs_0_, f32[3,3,512]{2,1,0:T(4,128)} %refs_1_.7, f32[8,512]{1,0:T(8,128)} %get-tuple-element.38.refs_2_, f32[3,128,512]{2,1,0:T(8,128)} %get-tuple-element.35.refs_4_.refs_3_, ...), custom_call_target="tpu_custom_call" | custom-call | bytes 2295808 | tf_op jit(solution)/shard_map/pallas_call | solution.py:310
Async XLA Ops:
  3.0 17.7 %all-to-all-start = ((bf16[8,144,128]{2,1,0:T(8,128)(2,1)}), bf16[8,144,128]{2,1,0:T(8,128)(2,1)S(1)}, u32[]{:S(2)}, u32[]{:S(2)}) async-start(bf16[8,144,128]{2,1,0:T(8,128)(2,1)} %shard_map.95), calls=%async_computation | async-start | bytes 589824 | tf_op jit(solution)/shard_map/all_to_all | solution.py:803
  12.1 1.6 %collective-permute-start = (bf16[2,128,512]{2,1,0:T(8,128)(2,1)S(1)}, bf16[2,128,512]{2,1,0:T(8,128)(2,1)S(1)}, u32[]{:S(2)}, u32[]{:S(2)}) collective-permute-start(bf16[2,128,512]{2,1,0:T(8,128)(2,1)S(1)} %get-tuple-element.28), channel_id=1, source_target_pairs={{0,1},{1,0},{2,3},{3,2},{4,5},{5,4},{6,7},{7,6},{8,9},{9,8},{10,11... | collective-permute-start | bytes 786440 | tf_op jit(solution)/shard_map/ppermute | solution.py:799
  14.2 5.6 %collective-permute-start.1 = (bf16[128,512]{1,0:T(8,128)(2,1)S(1)}, bf16[128,512]{1,0:T(8,128)(2,1)S(1)}, u32[]{:S(2)}, u32[]{:S(2)}) collective-permute-start(bf16[128,512]{1,0:T(8,128)(2,1)S(1)} %get-tuple-element.30), channel_id=1, source_target_pairs={{0,2},{1,3},{2,0},{3,1},{4,6},{5,7},{6,4},{7,5},{8,10},{9,11},{10,... | collective-permute-start | bytes 393224 | tf_op jit(solution)/shard_map/ppermute | solution.py:799
  42.8 12.0 %all-to-all-start.2 = ((bf16[8,144,128]{2,1,0:T(8,128)(2,1)}), bf16[8,144,128]{2,1,0:T(8,128)(2,1)S(1)}, u32[]{:S(2)}, u32[]{:S(2)}) async-start(bf16[8,144,128]{2,1,0:T(8,128)(2,1)} %get-tuple-element.37), calls=%async_computation.2 | async-start | bytes 589824 | tf_op jit(solution)/shard_map/all_to_all | solution.py:803
  46.3 5.0 %collective-permute-start.3 = (bf16[128,512]{1,0:T(8,128)(2,1)S(1)}, bf16[128,512]{1,0:T(8,128)(2,1)S(1)}, u32[]{:S(2)}, u32[]{:S(2)}) collective-permute-start(bf16[128,512]{1,0:T(8,128)(2,1)S(1)} %get-tuple-element.36.refs_1_), channel_id=1, source_target_pairs={{0,2},{1,3},{2,0},{3,1},{4,6},{5,7},{6,4},{7,5},{8,10},{9,11},{10,... | collective-permute-start | bytes 393224 | tf_op jit(solution)/shard_map/ppermute | solution.py:799
  47.8 3.5 %collective-permute-start.2 = (bf16[128,512]{1,0:T(8,128)(2,1)S(1)}, bf16[128,512]{1,0:T(8,128)(2,1)S(1)}, u32[]{:S(2)}, u32[]{:S(2)}) collective-permute-start(bf16[128,512]{1,0:T(8,128)(2,1)S(1)} %get-tuple-element.36.refs_1_), channel_id=1, source_target_pairs={{0,1},{1,0},{2,3},{3,2},{4,5},{5,4},{6,7},{7,6},{8,9},{9,8},{10,11... | collective-permute-start | bytes 393224 | tf_op jit(solution)/shard_map/ppermute | solution.py:799
  51.3 1.3 %collective-permute-start.4 = (bf16[128,512]{1,0:T(8,128)(2,1)S(1)}, bf16[128,512]{1,0:T(8,128)(2,1)S(1)}, u32[]{:S(2)}, u32[]{:S(2)}) collective-permute-start(bf16[128,512]{1,0:T(8,128)(2,1)S(1)} %collective-permute-done.3.refs_3_), channel_id=1, source_target_pairs={{0,1},{1,0},{2,3},{3,2},{4,5},{5,4},{6,7},{7,6},{8,9},{9,8},{10,11... | collective-permute-start | bytes 393224 | tf_op jit(solution)/shard_map/ppermute | solution.py:799

commit v3 on v2

--- a/solution.py
+++ b/solution.py
@@ -697,9 +697,6 @@
     high, rest = halves(columns(grad_long))
     three = zip(two_sides(fh, high), two_sides(fl, high), two_sides(fh, rest))
     main = [x + y + z for x, y, z in three]
-    gate(grad_ref, stage.take(4)[0], *[stage.out(i) for i in (1, 2, 3)])
-    stage.give(2)
-    stage.give(3)
     sides = []
     for phase in range(PHASES):
         sides.append([both(lane_tile(x, phase % 2))[phase // 2] for x in main])
@@ -708,7 +705,10 @@
         k_re, k_im = saved_ref[2 * r], saved_ref[2 * r + 1]
         product.append((k_re * re + k_im * im, k_re * im - k_im * re))
     high, rest = halves(columns(back_values(product, twist)))
-    bh, bl = stage.take(3)[0], stage.take(3)[1]
+    gate(grad_ref, stage.take(3)[0], *[stage.out(i) for i in (1, 2, 3)])
+    stage.give(2)
+    stage.give(3)
+    bh, bl = stage.take(4)[0], stage.take(4)[1]
     times = mm(bh, high) + mm(bl, high) + mm(bh, rest)
 
     scale = 1.0 / math.sqrt(PHASES * quarter)
@@ -893,8 +893,8 @@
         Near(swapped),
         Near(saved),
         Near(tables_on),
+        Far(short, [(0, 1)]),
         tables_back,
-        Far(short, [(0, 1)]),
         flops=table_flops,
     )
     grad_recv = exchanged(send, "seq")

time: 57.6 us -> 56.6 us (0.983)
  Pallas kernels: 17.5 us -> 16.4 us
    pallas_call x9, Pallas kernels: 17.5 us -> 16.4 us  [call(): pl.pallas_call(functools.partial(staged, kernel, items, len(args)), out_s...]
where the time goes in v3:
time: 56.6 us; the launch traced here: 56 us
  Pallas kernels  16.4 us (29%)
  blocking collectives  15.9 us (28%)
  starting transfers between devices  13.9 us (25%)
  waiting for transfers between devices  9.09 us (16%)
  between operations  0.72 us (1%)
    pallas_call x9, Pallas kernels, call(): pl.pallas_call(functools.partial(staged, kernel, items, len(args)), out_s...  16.4 us
    all_to_all x1, blocking collectives, exchanged(): return lax.all_to_all(x, axis, split_axis=0, concat_axis=0, tiled=True)  15.9 us
    all_to_all x2, starting transfers between devices, exchanged(): return lax.all_to_all(x, axis, split_axis=0, concat_axis=0, tiled=True)  10.7 us
    ppermute x5, waiting for transfers between devices, partner(): lax.ppermute(x, axis, [(i, i ^ mask) for i in range(lax.axis_size(axis))])  7.99 us
    ppermute x5, starting transfers between devices, partner(): lax.ppermute(x, axis, [(i, i ^ mask) for i in range(lax.axis_size(axis))])  3.2 us
  transfers between devices with their start and end apart: 7, of which 5 were waited for; matrix products, arithmetic and copies ran while one was open for 0% of the time, Pallas kernels for 12%

profile of v3, /device:TPU:0, one launch (start us, length us, event | category | flops | bytes accessed | tf_op | source)
XLA Modules:
  0.0 56.0 jit_solution(13467087502967398400)
XLA Ops:
  0.6 2.4 %shard_map.95 = bf16[8,144,128]{2,1,0:T(8,128)(2,1)} custom-call(f32[3,3,512]{2,1,0:T(4,128)} %refs_1_.7, bf16[3,128,512]{2,1,0:T(8,128)(2,1)} %refs_0_.5, f32[128,512]{1,0:T(8,128)} %refs_2_.2), custom_call_target="tpu_custom_call" | custom-call | bytes 968704 | tf_op jit(solution)/shard_map/pallas_call | solution.py:310
  3.0 7.3 %all-to-all-start = ((bf16[8,144,128]{2,1,0:T(8,128)(2,1)}), bf16[8,144,128]{2,1,0:T(8,128)(2,1)S(1)}, u32[]{:S(2)}, u32[]{:S(2)}) async-start(bf16[8,144,128]{2,1,0:T(8,128)(2,1)} %shard_map.95), calls=%async_computation | async-start | bytes 589824 | tf_op jit(solution)/shard_map/all_to_all | solution.py:803
  10.3 1.8 %shard_map.94 = (bf16[2,128,512]{2,1,0:T(8,128)(2,1)S(1)}, bf16[2048,512]{1,0:T(8,128)(2,1)S(1)}, bf16[128,512]{1,0:T(8,128)(2,1)S(1)}) custom-call(bf16[128,512]{1,0:T(8,128)(2,1)} %refs_0_.3, bf16[2048,512]{1,0:T(8,128)(2,1)} %refs_1_.4), custom_call_target="tpu_custom_call" | custom-call | flops 134217728 | bytes 4718592 | tf_op jit(solution)/shard_map/pallas_call | solution.py:310
  12.1 0.1 collective-permute-start
  12.2 1.5 %collective-permute-done.refs_2_ = bf16[2,128,512]{2,1,0:T(8,128)(2,1)S(1)} collective-permute-done((bf16[2,128,512]{2,1,0:T(8,128)(2,1)S(1)}, bf16[2,128,512]{2,1,0:T(8,128)(2,1)S(1)}, u32[]{:S(2)}, u32[]{:S(2)}) %collective-permute-start) | collective-permute-done | bytes 262176 | tf_op jit(solution)/shard_map/ppermute | solution.py:799
  13.7 0.5 shard_map.97
  14.2 1.6 %collective-permute-start.1 = (bf16[128,512]{1,0:T(8,128)(2,1)S(1)}, bf16[128,512]{1,0:T(8,128)(2,1)S(1)}, u32[]{:S(2)}, u32[]{:S(2)}) collective-permute-start(bf16[128,512]{1,0:T(8,128)(2,1)S(1)} %get-tuple-element.30), channel_id=1, source_target_pairs={{0,2},{1,3},{2,0},{3,1},{4,6},{5,7},{6,4},{7,5},{8,10},{9,11},{10,... | collective-permute-start | bytes 393224 | tf_op jit(solution)/shard_map/ppermute | solution.py:799
  15.8 2.4 %shard_map.96 = (bf16[3,256,512]{2,1,0:T(8,128)(2,1)S(1)}, f32[3,3,512]{2,1,0:T(4,128)S(1)}, f32[1,512]{1,0:T(1,128)S(1)}, f32[128,512]{1,0:T(8,128)S(1)}, f32[3,128,512]{2,1,0:T(8,128)}) custom-call(bf16[3,128,512]{2,1,0:T(8,128)(2,1)} %refs_0_.5, f32[3,3,512]{2,1,0:T(4,128)} %refs_1_.7, bf16[8,256,512]{2,1,0:T(8,128)(2,1)} %constant.2.clone.refs_2_.refs_4_, ...), custom_call_target="tpu_custom_call" | custom-call | bytes 4366336 | tf_op jit(solution)/shard_map/pallas_call | solution.py:310
  18.2 1.7 %collective-permute-done.1.refs_1_ = bf16[128,512]{1,0:T(8,128)(2,1)S(1)} collective-permute-done((bf16[128,512]{1,0:T(8,128)(2,1)S(1)}, bf16[128,512]{1,0:T(8,128)(2,1)S(1)}, u32[]{:S(2)}, u32[]{:S(2)}) %collective-permute-start.1) | collective-permute-done | bytes 131104 | tf_op jit(solution)/shard_map/ppermute | solution.py:799
  19.8 1.0 %shard_map.98 = (bf16[8,80,128]{2,1,0:T(8,128)(2,1)}, f32[128,512]{1,0:T(8,128)}) custom-call(f32[128,512]{1,0:T(8,128)S(1)} %get-tuple-element.29.refs_0_, bf16[128,512]{1,0:T(8,128)(2,1)S(1)} %collective-permute-done.1.refs_1_, f32[128,512]{1,0:T(8,128)S(1)} %get-tuple-element.31.refs_2_), custom_call_target="tpu_custom_call" | custom-call | bytes 1081344 | tf_op jit(solution)/shard_map/pallas_call | solution.py:310
  20.8 0.0 all-to-all-done.refs_0_
  20.8 2.5 %shard_map.99 = (bf16[8,144,128]{2,1,0:T(8,128)(2,1)}, f32[11,256,128]{2,1,0:T(8,128)S(1)}) custom-call(bf16[8,144,128]{2,1,0:T(8,128)(2,1)S(1)} %all-to-all-done.refs_0_, f32[3,3,512]{2,1,0:T(4,128)S(1)} %get-tuple-element.24.refs_1_, f32[1,512]{1,0:T(1,128)S(1)} %get-tuple-element.25.refs_2_, bf16[3,256,512]{2,1,0:T(8,128)(2,1)S(1)} %get-tuple-element.26.refs_3_.refs_2_, ...), custom_call_target="tpu_custom_call" | custom-call | flops 805306368 | bytes 5099520 | tf_op jit(solution)/shard_map/pallas_call | solution.py:310
  23.3 15.9 %all_to_all.15.refs_0_ = bf16[8,144,128]{2,1,0:T(8,128)(2,1)S(1)} all-to-all(bf16[8,144,128]{2,1,0:T(8,128)(2,1)} %get-tuple-element.33), channel_id=1, replica_groups=mesh['seq'=8,'ch'=4] {'seq'}, dimensions={0} | all-to-all | bytes 589824 | tf_op jit(solution)/shard_map/all_to_all | solution.py:803
  39.1 2.6 %shard_map.100 = (bf16[8,144,128]{2,1,0:T(8,128)(2,1)}, bf16[128,512]{1,0:T(8,128)(2,1)S(1)}, f32[128,512]{1,0:T(8,128)}, f32[8,512]{1,0:T(8,128)}) custom-call(bf16[8,144,128]{2,1,0:T(8,128)(2,1)S(1)} %all_to_all.15.refs_0_, f32[11,256,128]{2,1,0:T(8,128)S(1)} %get-tuple-element.34.refs_1_, bf16[3,256,512]{2,1,0:T(8,128)(2,1)S(1)} %get-tuple-element.26.refs_3_.refs_2_, ...), custom_call_target="tpu_custom_call" | custom-call | flops 805306368 | bytes 6111232 | tf_op jit(solution)/shard_map/pallas_call | solution.py:310
  41.8 3.4 %all-to-all-start.2 = ((bf16[8,144,128]{2,1,0:T(8,128)(2,1)}), bf16[8,144,128]{2,1,0:T(8,128)(2,1)S(1)}, u32[]{:S(2)}, u32[]{:S(2)}) async-start(bf16[8,144,128]{2,1,0:T(8,128)(2,1)} %get-tuple-element.37), calls=%async_computation.2 | async-start | bytes 589824 | tf_op jit(solution)/shard_map/all_to_all | solution.py:803
  45.2 1.6 %collective-permute-start.3 = (bf16[128,512]{1,0:T(8,128)(2,1)S(1)}, bf16[128,512]{1,0:T(8,128)(2,1)S(1)}, u32[]{:S(2)}, u32[]{:S(2)}) collective-permute-start(bf16[128,512]{1,0:T(8,128)(2,1)S(1)} %get-tuple-element.36.refs_1_), channel_id=1, source_target_pairs={{0,2},{1,3},{2,0},{3,1},{4,6},{5,7},{6,4},{7,5},{8,10},{9,11},{10,... | collective-permute-start | bytes 393224 | tf_op jit(solution)/shard_map/ppermute | solution.py:799
  46.8 0.0 collective-permute-start.2
  46.8 3.5 %collective-permute-done.3.refs_3_ = bf16[128,512]{1,0:T(8,128)(2,1)S(1)} collective-permute-done((bf16[128,512]{1,0:T(8,128)(2,1)S(1)}, bf16[128,512]{1,0:T(8,128)(2,1)S(1)}, u32[]{:S(2)}, u32[]{:S(2)}) %collective-permute-start.3) | collective-permute-done | bytes 131104 | tf_op jit(solution)/shard_map/ppermute | solution.py:799
  50.3 0.0 collective-permute-start.4
  50.3 0.0 collective-permute-done.2.refs_2_
  50.3 1.3 %collective-permute-done.4.refs_4_ = bf16[128,512]{1,0:T(8,128)(2,1)S(1)} collective-permute-done((bf16[128,512]{1,0:T(8,128)(2,1)S(1)}, bf16[128,512]{1,0:T(8,128)(2,1)S(1)}, u32[]{:S(2)}, u32[]{:S(2)}) %collective-permute-start.4) | collective-permute-done | bytes 131104 | tf_op jit(solution)/shard_map/ppermute | solution.py:799
  51.6 1.1 %shard_map.101 = bf16[128,512]{1,0:T(8,128)(2,1)} custom-call(bf16[2048,512]{1,0:T(8,128)(2,1)S(1)} %get-tuple-element.23.refs_1_.refs_0_, bf16[128,512]{1,0:T(8,128)(2,1)S(1)} %get-tuple-element.36.refs_1_, bf16[128,512]{1,0:T(8,128)(2,1)S(1)} %collective-permute-done.2.refs_2_, bf16[128,512]{1,0:T(8,128)(2,1)S(1)} %collective-permute-done.3.refs_3_, ...), custom_call_target="tpu_custom_call" | custom-call | flops 268435456 | bytes 2752512 | tf_op jit(solution)/shard_map/pallas_call | solution.py:310
  52.7 1.1 %all-to-all-done.2.refs_0_ = bf16[8,144,128]{2,1,0:T(8,128)(2,1)S(1)} async-done(((bf16[8,144,128]{2,1,0:T(8,128)(2,1)}), bf16[8,144,128]{2,1,0:T(8,128)(2,1)S(1)}, u32[]{:S(2)}, u32[]{:S(2)}) %all-to-all-start.2) | async-done | bytes 294944 | tf_op jit(solution)/shard_map/all_to_all | solution.py:803
  53.8 2.2 %shard_map.102 = (bf16[3,128,512]{2,1,0:T(8,128)(2,1)}, f32[128,512]{1,0:T(8,128)}) custom-call(bf16[8,144,128]{2,1,0:T(8,128)(2,1)S(1)} %all-to-all-done.2.refs_0_, f32[3,3,512]{2,1,0:T(4,128)} %refs_1_.7, f32[8,512]{1,0:T(8,128)} %get-tuple-element.38.refs_2_, f32[3,128,512]{2,1,0:T(8,128)} %get-tuple-element.35.refs_3_, ...), custom_call_target="tpu_custom_call" | custom-call | bytes 2295808 | tf_op jit(solution)/shard_map/pallas_call | solution.py:310
Async XLA Ops:
  3.0 17.7 %all-to-all-start = ((bf16[8,144,128]{2,1,0:T(8,128)(2,1)}), bf16[8,144,128]{2,1,0:T(8,128)(2,1)S(1)}, u32[]{:S(2)}, u32[]{:S(2)}) async-start(bf16[8,144,128]{2,1,0:T(8,128)(2,1)} %shard_map.95), calls=%async_computation | async-start | bytes 589824 | tf_op jit(solution)/shard_map/all_to_all | solution.py:803
  12.1 1.6 %collective-permute-start = (bf16[2,128,512]{2,1,0:T(8,128)(2,1)S(1)}, bf16[2,128,512]{2,1,0:T(8,128)(2,1)S(1)}, u32[]{:S(2)}, u32[]{:S(2)}) collective-permute-start(bf16[2,128,512]{2,1,0:T(8,128)(2,1)S(1)} %get-tuple-element.28), channel_id=1, source_target_pairs={{0,1},{1,0},{2,3},{3,2},{4,5},{5,4},{6,7},{7,6},{8,9},{9,8},{10,11... | collective-permute-start | bytes 786440 | tf_op jit(solution)/shard_map/ppermute | solution.py:799
  14.2 5.6 %collective-permute-start.1 = (bf16[128,512]{1,0:T(8,128)(2,1)S(1)}, bf16[128,512]{1,0:T(8,128)(2,1)S(1)}, u32[]{:S(2)}, u32[]{:S(2)}) collective-permute-start(bf16[128,512]{1,0:T(8,128)(2,1)S(1)} %get-tuple-element.30), channel_id=1, source_target_pairs={{0,2},{1,3},{2,0},{3,1},{4,6},{5,7},{6,4},{7,5},{8,10},{9,11},{10,... | collective-permute-start | bytes 393224 | tf_op jit(solution)/shard_map/ppermute | solution.py:799
  41.8 12.0 %all-to-all-start.2 = ((bf16[8,144,128]{2,1,0:T(8,128)(2,1)}), bf16[8,144,128]{2,1,0:T(8,128)(2,1)S(1)}, u32[]{:S(2)}, u32[]{:S(2)}) async-start(bf16[8,144,128]{2,1,0:T(8,128)(2,1)} %get-tuple-element.37), calls=%async_computation.2 | async-start | bytes 589824 | tf_op jit(solution)/shard_map/all_to_all | solution.py:803
  45.2 5.0 %collective-permute-start.3 = (bf16[128,512]{1,0:T(8,128)(2,1)S(1)}, bf16[128,512]{1,0:T(8,128)(2,1)S(1)}, u32[]{:S(2)}, u32[]{:S(2)}) collective-permute-start(bf16[128,512]{1,0:T(8,128)(2,1)S(1)} %get-tuple-element.36.refs_1_), channel_id=1, source_target_pairs={{0,2},{1,3},{2,0},{3,1},{4,6},{5,7},{6,4},{7,5},{8,10},{9,11},{10,... | collective-permute-start | bytes 393224 | tf_op jit(solution)/shard_map/ppermute | solution.py:799
  46.8 3.5 %collective-permute-start.2 = (bf16[128,512]{1,0:T(8,128)(2,1)S(1)}, bf16[128,512]{1,0:T(8,128)(2,1)S(1)}, u32[]{:S(2)}, u32[]{:S(2)}) collective-permute-start(bf16[128,512]{1,0:T(8,128)(2,1)S(1)} %get-tuple-element.36.refs_1_), channel_id=1, source_target_pairs={{0,1},{1,0},{2,3},{3,2},{4,5},{5,4},{6,7},{7,6},{8,9},{9,8},{10,11... | collective-permute-start | bytes 393224 | tf_op jit(solution)/shard_map/ppermute | solution.py:799
  50.3 1.3 %collective-permute-start.4 = (bf16[128,512]{1,0:T(8,128)(2,1)S(1)}, bf16[128,512]{1,0:T(8,128)(2,1)S(1)}, u32[]{:S(2)}, u32[]{:S(2)}) collective-permute-start(bf16[128,512]{1,0:T(8,128)(2,1)S(1)} %collective-permute-done.3.refs_3_), channel_id=1, source_target_pairs={{0,1},{1,0},{2,3},{3,2},{4,5},{5,4},{6,7},{7,6},{8,9},{9,8},{10,11... | collective-permute-start | bytes 393224 | tf_op jit(solution)/shard_map/ppermute | solution.py:799

commit v4 on v3

--- a/solution.py
+++ b/solution.py
@@ -759,14 +759,21 @@
     gated_ref[:STRIP, :] = (first * long_out[:STRIP]).astype(BF16)
 
 
-def output_kernel(parts, stage):
+def early_output_kernel(parts, stage):
     w_ref, total = stage.take(0), None
     for part in range(parts):
         gated = stage.take(1 + part)[...]
         width = gated.shape[1]
         term = mm(gated, w_ref[part * width : (part + 1) * width, :])
         total = term if total is None else total + term
-    stage.out(0)[...] = total.astype(BF16)
+    stage.out(0)[...] = total
+
+
+def output_kernel(part, stage):
+    gated = stage.take(1)[...]
+    width = gated.shape[1]
+    term = mm(gated, stage.take(0)[part * width : (part + 1) * width, :])
+    stage.out(0)[...] = (stage.take(2)[...] + term).astype(BF16)
 
 
 def end_kernel(stage):
@@ -900,15 +907,22 @@
     grad_recv = exchanged(send, "seq")
     across = partner(gated, "ch", 2)
     near, far = partner(gated, "ch", 1), partner(across, "ch", 1)
-    (output,) = call(
-        functools.partial(output_kernel, ch_parts),
-        [Far(column)],
+    (early,) = call(
+        functools.partial(early_output_kernel, ch_parts - 1),
+        [pinned(exact)],
         Near(w_kept),
         Near(gated),
         Near(near),
         Near(across),
+        flops=product_flops * (ch_parts - 1) // ch_parts,
+    )
+    (output,) = call(
+        functools.partial(output_kernel, ch_parts - 1),
+        [Far(column)],
+        Near(w_kept),
         Near(far),
-        flops=product_flops,
+        Near(early),
+        flops=product_flops // ch_parts,
     )
     grad_qkv, grad_filter = call(
         end_kernel,

time: 56.6 us -> 56.6 us (level)
    pallas_call x9 -> x10, Pallas kernels: 16.4 us -> 16.6 us  [call(): pl.pallas_call(functools.partial(staged, kernel, items, len(args)), out_s...]
where the time goes in v4:
time: 56.6 us; the launch traced here: 56 us
  Pallas kernels  16.6 us (29%)
  blocking collectives  15.9 us (28%)
  starting transfers between devices  13.9 us (25%)
  waiting for transfers between devices  8.91 us (16%)
  between operations  0.73 us (1%)
    pallas_call x10, Pallas kernels, call(): pl.pallas_call(functools.partial(staged, kernel, items, len(args)), out_s...  16.6 us
    all_to_all x1, blocking collectives, exchanged(): return lax.all_to_all(x, axis, split_axis=0, concat_axis=0, tiled=True)  15.9 us
    all_to_all x2, starting transfers between devices, exchanged(): return lax.all_to_all(x, axis, split_axis=0, concat_axis=0, tiled=True)  10.7 us
    ppermute x5, waiting for transfers between devices, partner(): lax.ppermute(x, axis, [(i, i ^ mask) for i in range(lax.axis_size(axis))])  7.6 us
    ppermute x5, starting transfers between devices, partner(): lax.ppermute(x, axis, [(i, i ^ mask) for i in range(lax.axis_size(axis))])  3.2 us
    all_to_all x2, waiting for transfers between devices, exchanged(): return lax.all_to_all(x, axis, split_axis=0, concat_axis=0, tiled=True)  1.31 us
  transfers between devices with their start and end apart: 7, of which 5 were waited for; matrix products, arithmetic and copies ran while one was open for 0% of the time, Pallas kernels for 12%

profile of v4, /device:TPU:0, one launch (start us, length us, event | category | flops | bytes accessed | tf_op | source)
XLA Modules:
  0.0 56.0 jit_solution(6606743849273413405)
XLA Ops:
  0.6 2.4 %shard_map.95 = bf16[8,144,128]{2,1,0:T(8,128)(2,1)} custom-call(f32[3,3,512]{2,1,0:T(4,128)} %refs_1_.7, bf16[3,128,512]{2,1,0:T(8,128)(2,1)} %refs_0_.5, f32[128,512]{1,0:T(8,128)} %refs_2_.2), custom_call_target="tpu_custom_call" | custom-call | bytes 968704 | tf_op jit(solution)/shard_map/pallas_call | solution.py:310
  3.0 7.3 %all-to-all-start = ((bf16[8,144,128]{2,1,0:T(8,128)(2,1)}), bf16[8,144,128]{2,1,0:T(8,128)(2,1)S(1)}, u32[]{:S(2)}, u32[]{:S(2)}) async-start(bf16[8,144,128]{2,1,0:T(8,128)(2,1)} %shard_map.95), calls=%async_computation | async-start | bytes 589824 | tf_op jit(solution)/shard_map/all_to_all | solution.py:810
  10.3 1.8 %shard_map.94 = (bf16[2,128,512]{2,1,0:T(8,128)(2,1)S(1)}, bf16[2048,512]{1,0:T(8,128)(2,1)S(1)}, bf16[128,512]{1,0:T(8,128)(2,1)S(1)}) custom-call(bf16[128,512]{1,0:T(8,128)(2,1)} %refs_0_.3, bf16[2048,512]{1,0:T(8,128)(2,1)} %refs_1_.4), custom_call_target="tpu_custom_call" | custom-call | flops 134217728 | bytes 4718592 | tf_op jit(solution)/shard_map/pallas_call | solution.py:310
  12.1 0.1 collective-permute-start
  12.2 1.5 %collective-permute-done.refs_2_ = bf16[2,128,512]{2,1,0:T(8,128)(2,1)S(1)} collective-permute-done((bf16[2,128,512]{2,1,0:T(8,128)(2,1)S(1)}, bf16[2,128,512]{2,1,0:T(8,128)(2,1)S(1)}, u32[]{:S(2)}, u32[]{:S(2)}) %collective-permute-start) | collective-permute-done | bytes 262176 | tf_op jit(solution)/shard_map/ppermute | solution.py:806
  13.7 0.5 shard_map.97
  14.2 1.6 %collective-permute-start.1 = (bf16[128,512]{1,0:T(8,128)(2,1)S(1)}, bf16[128,512]{1,0:T(8,128)(2,1)S(1)}, u32[]{:S(2)}, u32[]{:S(2)}) collective-permute-start(bf16[128,512]{1,0:T(8,128)(2,1)S(1)} %get-tuple-element.30), channel_id=1, source_target_pairs={{0,2},{1,3},{2,0},{3,1},{4,6},{5,7},{6,4},{7,5},{8,10},{9,11},{10,... | collective-permute-start | bytes 393224 | tf_op jit(solution)/shard_map/ppermute | solution.py:806
  15.8 2.4 %shard_map.96 = (bf16[3,256,512]{2,1,0:T(8,128)(2,1)S(1)}, f32[3,3,512]{2,1,0:T(4,128)S(1)}, f32[1,512]{1,0:T(1,128)S(1)}, f32[128,512]{1,0:T(8,128)S(1)}, f32[3,128,512]{2,1,0:T(8,128)}) custom-call(bf16[3,128,512]{2,1,0:T(8,128)(2,1)} %refs_0_.5, f32[3,3,512]{2,1,0:T(4,128)} %refs_1_.7, bf16[8,256,512]{2,1,0:T(8,128)(2,1)} %constant.2.clone.refs_2_.refs_4_, ...), custom_call_target="tpu_custom_call" | custom-call | bytes 4366336 | tf_op jit(solution)/shard_map/pallas_call | solution.py:310
  18.2 1.7 %collective-permute-done.1.refs_1_ = bf16[128,512]{1,0:T(8,128)(2,1)S(1)} collective-permute-done((bf16[128,512]{1,0:T(8,128)(2,1)S(1)}, bf16[128,512]{1,0:T(8,128)(2,1)S(1)}, u32[]{:S(2)}, u32[]{:S(2)}) %collective-permute-start.1) | collective-permute-done | bytes 131104 | tf_op jit(solution)/shard_map/ppermute | solution.py:806
  19.8 1.0 %shard_map.98 = (bf16[8,80,128]{2,1,0:T(8,128)(2,1)}, f32[128,512]{1,0:T(8,128)}) custom-call(f32[128,512]{1,0:T(8,128)S(1)} %get-tuple-element.29.refs_0_, bf16[128,512]{1,0:T(8,128)(2,1)S(1)} %collective-permute-done.1.refs_1_, f32[128,512]{1,0:T(8,128)S(1)} %get-tuple-element.31.refs_2_), custom_call_target="tpu_custom_call" | custom-call | bytes 1081344 | tf_op jit(solution)/shard_map/pallas_call | solution.py:310
  20.8 0.0 all-to-all-done.refs_0_
  20.8 2.5 %shard_map.99 = (bf16[8,144,128]{2,1,0:T(8,128)(2,1)}, f32[11,256,128]{2,1,0:T(8,128)S(1)}) custom-call(bf16[8,144,128]{2,1,0:T(8,128)(2,1)S(1)} %all-to-all-done.refs_0_, f32[3,3,512]{2,1,0:T(4,128)S(1)} %get-tuple-element.24.refs_1_, f32[1,512]{1,0:T(1,128)S(1)} %get-tuple-element.25.refs_2_, bf16[3,256,512]{2,1,0:T(8,128)(2,1)S(1)} %get-tuple-element.26.refs_3_.refs_2_, ...), custom_call_target="tpu_custom_call" | custom-call | flops 805306368 | bytes 5099520 | tf_op jit(solution)/shard_map/pallas_call | solution.py:310
  23.3 15.9 %all_to_all.15.refs_0_ = bf16[8,144,128]{2,1,0:T(8,128)(2,1)S(1)} all-to-all(bf16[8,144,128]{2,1,0:T(8,128)(2,1)} %get-tuple-element.33), channel_id=1, replica_groups=mesh['seq'=8,'ch'=4] {'seq'}, dimensions={0} | all-to-all | bytes 589824 | tf_op jit(solution)/shard_map/all_to_all | solution.py:810
  39.1 2.6 %shard_map.100 = (bf16[8,144,128]{2,1,0:T(8,128)(2,1)}, bf16[128,512]{1,0:T(8,128)(2,1)S(1)}, f32[128,512]{1,0:T(8,128)}, f32[8,512]{1,0:T(8,128)}) custom-call(bf16[8,144,128]{2,1,0:T(8,128)(2,1)S(1)} %all_to_all.15.refs_0_, f32[11,256,128]{2,1,0:T(8,128)S(1)} %get-tuple-element.34.refs_1_, bf16[3,256,512]{2,1,0:T(8,128)(2,1)S(1)} %get-tuple-element.26.refs_3_.refs_2_, ...), custom_call_target="tpu_custom_call" | custom-call | flops 805306368 | bytes 6111232 | tf_op jit(solution)/shard_map/pallas_call | solution.py:310
  41.8 3.4 %all-to-all-start.2 = ((bf16[8,144,128]{2,1,0:T(8,128)(2,1)}), bf16[8,144,128]{2,1,0:T(8,128)(2,1)S(1)}, u32[]{:S(2)}, u32[]{:S(2)}) async-start(bf16[8,144,128]{2,1,0:T(8,128)(2,1)} %get-tuple-element.37), calls=%async_computation.2 | async-start | bytes 589824 | tf_op jit(solution)/shard_map/all_to_all | solution.py:810
  45.2 1.6 %collective-permute-start.2 = (bf16[128,512]{1,0:T(8,128)(2,1)S(1)}, bf16[128,512]{1,0:T(8,128)(2,1)S(1)}, u32[]{:S(2)}, u32[]{:S(2)}) collective-permute-start(bf16[128,512]{1,0:T(8,128)(2,1)S(1)} %get-tuple-element.36.refs_1_), channel_id=1, source_target_pairs={{0,2},{1,3},{2,0},{3,1},{4,6},{5,7},{6,4},{7,5},{8,10},{9,11},{10,... | collective-permute-start | bytes 393224 | tf_op jit(solution)/shard_map/ppermute | solution.py:806
  46.8 0.0 collective-permute-start.4
  46.8 3.5 %collective-permute-done.2.refs_3_ = bf16[128,512]{1,0:T(8,128)(2,1)S(1)} collective-permute-done((bf16[128,512]{1,0:T(8,128)(2,1)S(1)}, bf16[128,512]{1,0:T(8,128)(2,1)S(1)}, u32[]{:S(2)}, u32[]{:S(2)}) %collective-permute-start.2) | collective-permute-done | bytes 131104 | tf_op jit(solution)/shard_map/ppermute | solution.py:806
  50.3 0.0 collective-permute-start.3
  50.3 0.0 collective-permute-done.4.refs_2_
  50.3 0.4 shard_map.101.refs_2_
  50.7 0.9 %collective-permute-done.3.refs_1_ = bf16[128,512]{1,0:T(8,128)(2,1)S(1)} collective-permute-done((bf16[128,512]{1,0:T(8,128)(2,1)S(1)}, bf16[128,512]{1,0:T(8,128)(2,1)S(1)}, u32[]{:S(2)}, u32[]{:S(2)}) %collective-permute-start.3) | collective-permute-done | bytes 131104 | tf_op jit(solution)/shard_map/ppermute | solution.py:806
  51.6 0.9 %shard_map.102 = bf16[128,512]{1,0:T(8,128)(2,1)} custom-call(bf16[2048,512]{1,0:T(8,128)(2,1)S(1)} %get-tuple-element.23.refs_1_.refs_0_, bf16[128,512]{1,0:T(8,128)(2,1)S(1)} %collective-permute-done.3.refs_1_, f32[128,512]{1,0:T(8,128)S(1)} %shard_map.101.refs_2_), custom_call_target="tpu_custom_call" | custom-call | flops 67108864 | bytes 2621440 | tf_op jit(solution)/shard_map/pallas_call | solution.py:310
  52.5 1.3 %all-to-all-done.2.refs_0_ = bf16[8,144,128]{2,1,0:T(8,128)(2,1)S(1)} async-done(((bf16[8,144,128]{2,1,0:T(8,128)(2,1)}), bf16[8,144,128]{2,1,0:T(8,128)(2,1)S(1)}, u32[]{:S(2)}, u32[]{:S(2)}) %all-to-all-start.2) | async-done | bytes 294944 | tf_op jit(solution)/shard_map/all_to_all | solution.py:810
  53.8 2.2 %shard_map.103 = (bf16[3,128,512]{2,1,0:T(8,128)(2,1)}, f32[128,512]{1,0:T(8,128)}) custom-call(bf16[8,144,128]{2,1,0:T(8,128)(2,1)S(1)} %all-to-all-done.2.refs_0_, f32[3,3,512]{2,1,0:T(4,128)} %refs_1_.7, f32[8,512]{1,0:T(8,128)} %get-tuple-element.38.refs_2_, f32[3,128,512]{2,1,0:T(8,128)} %get-tuple-element.35.refs_3_, ...), custom_call_target="tpu_custom_call" | custom-call | bytes 2295808 | tf_op jit(solution)/shard_map/pallas_call | solution.py:310
Async XLA Ops:
  3.0 17.7 %all-to-all-start = ((bf16[8,144,128]{2,1,0:T(8,128)(2,1)}), bf16[8,144,128]{2,1,0:T(8,128)(2,1)S(1)}, u32[]{:S(2)}, u32[]{:S(2)}) async-start(bf16[8,144,128]{2,1,0:T(8,128)(2,1)} %shard_map.95), calls=%async_computation | async-start | bytes 589824 | tf_op jit(solution)/shard_map/all_to_all | solution.py:810
  12.1 1.6 %collective-permute-start = (bf16[2,128,512]{2,1,0:T(8,128)(2,1)S(1)}, bf16[2,128,512]{2,1,0:T(8,128)(2,1)S(1)}, u32[]{:S(2)}, u32[]{:S(2)}) collective-permute-start(bf16[2,128,512]{2,1,0:T(8,128)(2,1)S(1)} %get-tuple-element.28), channel_id=1, source_target_pairs={{0,1},{1,0},{2,3},{3,2},{4,5},{5,4},{6,7},{7,6},{8,9},{9,8},{10,11... | collective-permute-start | bytes 786440 | tf_op jit(solution)/shard_map/ppermute | solution.py:806
  14.2 5.6 %collective-permute-start.1 = (bf16[128,512]{1,0:T(8,128)(2,1)S(1)}, bf16[128,512]{1,0:T(8,128)(2,1)S(1)}, u32[]{:S(2)}, u32[]{:S(2)}) collective-permute-start(bf16[128,512]{1,0:T(8,128)(2,1)S(1)} %get-tuple-element.30), channel_id=1, source_target_pairs={{0,2},{1,3},{2,0},{3,1},{4,6},{5,7},{6,4},{7,5},{8,10},{9,11},{10,... | collective-permute-start | bytes 393224 | tf_op jit(solution)/shard_map/ppermute | solution.py:806
  41.8 12.0 %all-to-all-start.2 = ((bf16[8,144,128]{2,1,0:T(8,128)(2,1)}), bf16[8,144,128]{2,1,0:T(8,128)(2,1)S(1)}, u32[]{:S(2)}, u32[]{:S(2)}) async-start(bf16[8,144,128]{2,1,0:T(8,128)(2,1)} %get-tuple-element.37), calls=%async_computation.2 | async-start | bytes 589824 | tf_op jit(solution)/shard_map/all_to_all | solution.py:810
  45.2 5.0 %collective-permute-start.2 = (bf16[128,512]{1,0:T(8,128)(2,1)S(1)}, bf16[128,512]{1,0:T(8,128)(2,1)S(1)}, u32[]{:S(2)}, u32[]{:S(2)}) collective-permute-start(bf16[128,512]{1,0:T(8,128)(2,1)S(1)} %get-tuple-element.36.refs_1_), channel_id=1, source_target_pairs={{0,2},{1,3},{2,0},{3,1},{4,6},{5,7},{6,4},{7,5},{8,10},{9,11},{10,... | collective-permute-start | bytes 393224 | tf_op jit(solution)/shard_map/ppermute | solution.py:806
  46.8 3.5 %collective-permute-start.4 = (bf16[128,512]{1,0:T(8,128)(2,1)S(1)}, bf16[128,512]{1,0:T(8,128)(2,1)S(1)}, u32[]{:S(2)}, u32[]{:S(2)}) collective-permute-start(bf16[128,512]{1,0:T(8,128)(2,1)S(1)} %get-tuple-element.36.refs_1_), channel_id=1, source_target_pairs={{0,1},{1,0},{2,3},{3,2},{4,5},{5,4},{6,7},{7,6},{8,9},{9,8},{10,11... | collective-permute-start | bytes 393224 | tf_op jit(solution)/shard_map/ppermute | solution.py:806
  50.3 1.3 %collective-permute-start.3 = (bf16[128,512]{1,0:T(8,128)(2,1)S(1)}, bf16[128,512]{1,0:T(8,128)(2,1)S(1)}, u32[]{:S(2)}, u32[]{:S(2)}) collective-permute-start(bf16[128,512]{1,0:T(8,128)(2,1)S(1)} %collective-permute-done.2.refs_3_), channel_id=1, source_target_pairs={{0,1},{1,0},{2,3},{3,2},{4,5},{5,4},{6,7},{7,6},{8,9},{9,8},{10,11... | collective-permute-start | bytes 393224 | tf_op jit(solution)/shard_map/ppermute | solution.py:806
